TPU v7x, 256 devices: a whole 4x4x8 slice. The times are simulated.
256 devices in a mesh: role: 8 (over z), seq: 32 (over x, y, core).
Axes of the slice: x: 4, y: 4, z: 8, core: 2. Of those that a mesh axis runs over, the one named last changes fastest.
Arguments:
- prefill_queries: bfloat16 [8, 4096, 8192], P('role', 'seq'), may hold values from -140 to 140
- prefill_kv: bfloat16 [8, 4096, 2048], P('role', 'seq'), may hold values from -13 to 13
- prompt_lengths: int32 [4, 4], replicated, may hold values from 1 to 2048, as said below
- decode_group: int32 [4, 4], replicated, may hold values from 0 to 3, as said below
- decode_queries: bfloat16 [8, 4, 4, 8192], P('role', None, None, 'seq'), may hold values from -140 to 140
- decode_kv: bfloat16 [8, 4, 4, 2048], P('role'), may hold values from -13 to 13
- out_weight: bfloat16 [8192, 8192], P('seq'), may hold values from -0.125 to 0.125
Outputs:
- prefill_out: bfloat16 [8, 4096, 8192], P('role', 'seq')
- decode_out: bfloat16 [4, 4, 4, 8192], replicated
Inputs may be any that keep to these rules, and one draw needn't show every extreme that they name: `prompt_lengths`: in each row the block counts ceil(length / 128) sum to 32 and are at most 16; each row has a request of exactly 16 blocks whose length is 2048. `decode_group`: each row is a permutation of 0 to 3.
All inputs are finite; a program needn't handle non-finite values.
Results may differ from a plain program's by a relative error of at most 0.006.
Values may be sent and summed in bfloat16 or wider, within the bound.
A program may use at most 128 MiB of HBM per device.

v0:
```python
import jax
import jax.numpy as jnp
from jax import lax
from jax.sharding import PartitionSpec as P

H = 64
KVH = 8
HD = 128
BLOCK = 128


def for_sending(array):
    return jax.tree.map(lambda a: a.astype(jnp.bfloat16) if a.dtype == jnp.float32 else a, array)


def request_layout(lengths, span_rows):
    blocks = (lengths + BLOCK - 1) // BLOCK
    starts = (jnp.cumsum(blocks) - blocks) * BLOCK
    position = jnp.arange(span_rows, dtype=jnp.int32)
    member = starts[None, :] <= position[:, None]
    segment = jnp.sum(member.astype(jnp.int32), axis=1) - 1
    owning = segment[:, None] == jnp.arange(lengths.shape[0], dtype=jnp.int32)[None, :]
    opening = jnp.sum(jnp.where(owning, starts[None, :], 0), axis=1)
    ceiling = jnp.sum(jnp.where(owning, lengths[None, :], 0), axis=1)
    return (segment, position - opening < ceiling, starts)


def prefill_attention(head_queries, head_cache, lengths):
    span_rows = head_cache.shape[0]
    local_heads = head_queries.shape[1] // HD
    segment, live_rows, starts = request_layout(lengths, span_rows)
    position = jnp.arange(span_rows, dtype=jnp.int32)
    queries = head_queries.reshape(span_rows, local_heads, HD)
    keys_all = head_cache[:, :HD]
    values_all = head_cache[:, HD:]
    step_rows = min(512, span_rows)
    results = []
    for block_number in range(span_rows // step_rows):
        row_start = block_number * step_rows
        row_stop = row_start + step_rows
        scores = jnp.einsum(
            "qhd,kd->qhk",
            queries[row_start:row_stop],
            keys_all[:row_stop],
            preferred_element_type=jnp.float32,
        ) * HD ** (-0.5)
        allowed = (
            (segment[row_start:row_stop, None] == segment[None, :row_stop])
            & (position[None, :row_stop] <= position[row_start:row_stop, None])
            & live_rows[None, :row_stop]
        )
        scores = jnp.where(allowed[:, None, :], scores, -jnp.inf)
        weights = jnp.exp(scores - jnp.max(scores, axis=2, keepdims=True))
        weights = (weights / jnp.sum(weights, axis=2, keepdims=True)).astype(jnp.bfloat16)
        mixed_rows = jnp.einsum(
            "qhk,kd->qhd", weights, values_all[:row_stop], preferred_element_type=jnp.float32
        )
        mixed_rows = jnp.where(live_rows[row_start:row_stop, None, None], mixed_rows, 0.0)
        results.append(mixed_rows.astype(jnp.bfloat16).reshape(step_rows, local_heads * HD))
    return jnp.concatenate(results, axis=0)


def decode_terms(
    cached, decode_queries, decode_kv, out_weight, prompt_lengths, decode_group, target, kv_head
):
    groups_in = prompt_lengths.shape[0]
    capacity = cached.shape[1]
    steps_count = decode_queries.shape[1]
    local_heads = decode_queries.shape[3] // HD
    matched = decode_group == target
    limits = jnp.sum(jnp.where(matched, prompt_lengths, 0), axis=1)
    query_rows = decode_queries[0].reshape(steps_count, groups_in, local_heads, HD)
    arrivals = lax.dynamic_slice_in_dim(decode_kv[0], kv_head * 2 * HD, 2 * HD, 2)
    score_scale = HD ** (-0.5)
    cached_scores = (
        jnp.einsum(
            "sphd,pcd->phsc", query_rows, cached[:, :, :HD], preferred_element_type=jnp.float32
        )
        * score_scale
    )
    live_keys = jnp.arange(capacity, dtype=jnp.int32)[None, :] < limits[:, None]
    cached_scores = jnp.where(live_keys[:, None, None, :], cached_scores, -jnp.inf)
    fresh_scores = (
        jnp.einsum(
            "sphd,tpd->phst", query_rows, arrivals[:, :, :HD], preferred_element_type=jnp.float32
        )
        * score_scale
    )
    causal = jnp.arange(steps_count)[None, :] <= jnp.arange(steps_count)[:, None]
    fresh_scores = jnp.where(causal, fresh_scores, -jnp.inf)
    scores = jnp.concatenate([cached_scores, fresh_scores], axis=3)
    weights = jnp.exp(scores - jnp.max(scores, axis=3, keepdims=True))
    weights = (weights / jnp.sum(weights, axis=3, keepdims=True)).astype(jnp.bfloat16)
    mixed_heads = jnp.einsum(
        "phsc,pcd->sphd",
        weights[..., :capacity],
        cached[:, :, HD:],
        preferred_element_type=jnp.float32,
    )
    mixed_heads = mixed_heads + jnp.einsum(
        "phst,tpd->sphd",
        weights[..., capacity:],
        arrivals[:, :, HD:],
        preferred_element_type=jnp.float32,
    )
    attended = mixed_heads.astype(jnp.bfloat16).reshape(steps_count, groups_in, local_heads * HD)
    return jnp.einsum("spc,cd->spd", attended, out_weight, preferred_element_type=jnp.float32)


def on_device(
    prefill_queries, prefill_kv, prompt_lengths, decode_group, decode_queries, decode_kv, out_weight
):
    seq_count = lax.axis_size("seq")
    role_count = lax.axis_size("role")
    prefill_groups = role_count // 2
    role_index = lax.axis_index("role")
    seq_index = lax.axis_index("seq")
    copies = seq_count // KVH
    local_heads = H // seq_count
    span_rows = BLOCK * seq_count
    capacity = seq_count // 2 * BLOCK
    local_queries = prefill_queries[0].reshape(BLOCK, seq_count, local_heads * HD)
    local_cache = jnp.repeat(prefill_kv[0].reshape(BLOCK, KVH, 2 * HD), copies, axis=1)
    head_queries, head_cache = (
        lax.all_to_all(local_queries, "seq", split_axis=1, concat_axis=0, tiled=True),
        lax.all_to_all(local_cache, "seq", split_axis=1, concat_axis=0, tiled=True),
    )
    head_queries = head_queries.reshape(span_rows, local_heads * HD)
    head_cache = head_cache.reshape(span_rows, 2 * HD)
    own_group = jnp.minimum(role_index, prefill_groups - 1)
    own_lengths = prompt_lengths[own_group]
    blocks = (own_lengths + BLOCK - 1) // BLOCK
    starts = (jnp.cumsum(blocks) - blocks) * BLOCK
    matched = (
        decode_group[own_group][None, :] == jnp.arange(prefill_groups, dtype=jnp.int32)[:, None]
    )
    openings = jnp.sum(jnp.where(matched, starts[None, :], 0), axis=1)
    padded = jnp.concatenate([head_cache, jnp.zeros((capacity, 2 * HD), jnp.bfloat16)], axis=0)
    place = (role_index - prefill_groups) % prefill_groups
    windows = jax.vmap(lambda opening: lax.dynamic_slice_in_dim(padded, opening, capacity, 0))(
        openings
    )
    outgoing = jnp.concatenate([jnp.zeros_like(windows), windows], axis=0)
    cached = lax.all_to_all(outgoing, "role", split_axis=0, concat_axis=0, tiled=True)[
        :prefill_groups
    ]
    attended = lax.cond(
        role_index < prefill_groups,
        lambda operands: prefill_attention(*operands),
        lambda operands: jnp.zeros((span_rows, local_heads * HD), jnp.bfloat16),
        (head_queries, head_cache, own_lengths),
    )
    returned = lax.all_to_all(
        for_sending(attended.reshape(seq_count, BLOCK, 1, local_heads * HD)),
        "seq",
        split_axis=0,
        concat_axis=2,
        tiled=True,
    )
    prefill_out = returned.reshape(1, BLOCK, H * HD)
    kv_head = seq_index // copies
    steps_count = decode_queries.shape[1]
    width = out_weight.shape[1]
    term_rows = lax.cond(
        role_index >= prefill_groups,
        lambda operands: decode_terms(*operands, prompt_lengths, decode_group, place, kv_head),
        lambda operands: jnp.zeros((steps_count, prefill_groups, width), jnp.float32),
        (cached, decode_queries, decode_kv, out_weight),
    )
    summed = lax.psum(term_rows, "seq").astype(jnp.bfloat16)
    decode_out = lax.all_gather(summed[:, None], "role", axis=1, tiled=True)[:, prefill_groups:]
    return (prefill_out, decode_out)


def solution(mesh):
    in_specs = (
        P("role", "seq", None),
        P("role", "seq", None),
        P(),
        P(),
        P("role", None, None, "seq"),
        P("role", None, None, None),
        P("seq", None),
    )
    out_specs = (P("role", "seq", None), P())
    return jax.shard_map(
        on_device, mesh=mesh, in_specs=in_specs, out_specs=out_specs, check_vma=False
    )
```

profile of v0, /device:TPU:1, one launch (start us, length us, event | category | flops | bytes accessed | tf_op | source)
XLA Modules:
  0.0 603.2 jit_solution(10297398569115466919)
XLA Ops:
  10.0 8.6 %all-to-all-start.1 = ((bf16[128,32,256]{2,0,1:T(8,128)(2,1)}), bf16[128,32,256]{2,0,1:T(8,128)(2,1)S(1)}, u32[]{:S(2)}, u32[]{:S(2)}) async-start(bf16[128,32,256]{2,0,1:T(8,128)(2,1)} %bitcast.280), calls=%async_computation.1 | async-start | bytes 4194304 | tf_op jit(solution)/shard_map/all_to_all | solution.py:126
  19.0 27.9 %all-to-all-done.1 = bf16[128,32,256]{2,0,1:T(8,128)(2,1)S(1)} async-done(((bf16[128,32,256]{2,0,1:T(8,128)(2,1)}), bf16[128,32,256]{2,0,1:T(8,128)(2,1)S(1)}, u32[]{:S(2)}, u32[]{:S(2)}) %all-to-all-start.1) | async-done | bytes 2097184 | tf_op jit(solution)/shard_map/all_to_all | solution.py:126
  50.0 10.0 %while.1 = (s32[]{:T(128)}, bf16[6144,256]{1,0:T(8,128)(2,1)S(1)}, s32[4,2]{0,1:T(2,128)S(1)}, bf16[4,2048,256]{2,1,0:T(8,128)(2,1)}, s32[]{:T(128)}) while((s32[]{:T(128)}, bf16[6144,256]{1,0:T(8,128)(2,1)S(1)}, s32[4,2]{0,1:T(2,128)S(1)}, bf16[4,2048,256]{2,1,0:T(8,128)(2,1)}, s32[]{:T(128)}) %tuple.96), condition=%wide.while_cond, body=%wide.while_body.sunk | while | flops 2 | bytes 2097765 | solution.py:140
  60.0 5.9 concatenate.21
  65.9 8.3 %all-to-all-start.3 = ((bf16[8,2048,256]{2,1,0:T(8,128)(2,1)}), bf16[8,2048,256]{2,1,0:T(8,128)(2,1)}, u32[]{:S(2)}, u32[]{:S(2)}) async-start(bf16[8,2048,256]{2,1,0:T(8,128)(2,1)} %concatenate.21), calls=%async_computation.3 | async-start | bytes 16777216 | tf_op jit(solution)/shard_map/all_to_all | solution.py:144
  76.7 184.6 %all-to-all-done.3 = bf16[8,2048,256]{2,1,0:T(8,128)(2,1)} async-done(((bf16[8,2048,256]{2,1,0:T(8,128)(2,1)}), bf16[8,2048,256]{2,1,0:T(8,128)(2,1)}, u32[]{:S(2)}, u32[]{:S(2)}) %all-to-all-start.3) | async-done | bytes 8388640 | tf_op jit(solution)/shard_map/all_to_all | solution.py:144
  261.3 4.8 all-to-all-start
  266.7 143.5 %all-reduce.4 = bf16[4,4,8192]{2,0,1:T(4,128)(2,1)} all-reduce(f32[4,4,8192]{2,0,1:T(4,128)S(1)} %copy.140), channel_id=1, replica_groups=mesh['role'=8,'seq'=32] {'seq'}, use_global_device_ids=true, to_apply=%region_30.31 | all-reduce | flops 131072 | bytes 786432 | tf_op jit(solution)/shard_map/psum | solution.py:170
  410.3 4.5 copy.134
  414.8 131.2 %conditional.2 = (bf16[4096,256]{0,1:T(8,128)(2,1)}) conditional(s32[]{:T(128)} %convert_element_type.74, () %tuple.31, (s32[1,4]{1,0:T(1,128)S(1)}, bf16[32,128,1,256]{3,0,1,2:T(8,128)(2,1)}, bf16[4096,256]{1,0:T(8,128)(2,1)S(1)}) %tuple.106), branch_computations={%region_0.1_spmd, %region_1.22_spmd} | conditional | flops 10903267328 | bytes 177283296 | solution.py:147
  420.2 3.2 fusion.265
  423.4 3.1 copy.114
  430.6 4.5 fusion.270
  435.1 3.2 fusion.58
  440.6 3.3 fusion.279
  443.9 4.0 fusion.60
  450.6 7.4 %fusion.284 = (f32[512,2]{0,1:T(2,128)S(1)}, f32[512,2,2048]{2,0,1:T(8,128)}) fusion(pred[512,2048]{1,0:T(8,128)(4,1)S(1)} %and_and_fusion.3, bf16[4096,256]{1,0:T(8,128)(2,1)S(1)} %get-tuple-element.253, bf16[512,2,128]{2,1,0:T(2,128)(2,1)} %slice.252), kind=kOutput, calls=%fused_computation.277 | convolution fusion | flops 545261568 | bytes 10227712 | tf_op jit(solution)/shard_map/cond/branch_1_fun/sub | solution.py:53
  458.0 5.0 fusion.56
  467.5 4.8 fusion.293
  472.3 6.0 fusion.62
  480.0 3.1 and_and_fusion.1
  484.1 8.4 %fusion.298 = (f32[512,2]{0,1:T(2,128)S(1)}, f32[512,2,3072]{2,0,1:T(8,128)}) fusion(pred[512,3072]{1,0:T(8,128)(4,1)} %and_and_fusion.1, bf16[4096,256]{1,0:T(8,128)(2,1)S(1)} %get-tuple-element.253, bf16[512,2,128]{2,1,0:T(2,128)(2,1)S(1)} %slice.272), kind=kOutput, calls=%fused_computation.279 | convolution fusion | flops 817892352 | bytes 15208448 | tf_op jit(solution)/shard_map/cond/branch_1_fun/sub | solution.py:53
  492.5 7.0 %fusion.54 = bf16[512,2,128]{0,2,1:T(8,128)(2,1)S(1)} fusion(f32[512,2,3072]{2,0,1:T(8,128)} %get-tuple-element.412, f32[512,2]{0,1:T(2,128)S(1)} %get-tuple-element.411, bf16[4096,256]{0,1:T(8,128)(2,1)} %copy.114, pred[512]{0:T(512)(128)(4,1)S(1)} %get-tuple-element.399), kind=kOutput, calls=%fused_computation.83 | convolution fusion | flops 811859968 | bytes 13636096 | tf_op jit(solution)/shard_map/cond/branch_1_fun/qhk,kd->qhd/dot_general | solution.py:55
  500.3 2.9 and_and_fusion
  503.3 9.6 %fusion.307 = (f32[512,2]{0,1:T(2,128)S(1)}, f32[512,2,3584]{2,0,1:T(8,128)}) fusion(pred[512,3584]{1,0:T(8,128)(4,1)} %and_and_fusion, bf16[4096,256]{1,0:T(8,128)(2,1)S(1)} %get-tuple-element.253, bf16[512,2,128]{2,1,0:T(2,128)(2,1)S(1)} %slice.282), kind=kOutput, calls=%fused_computation.280 | convolution fusion | flops 954207744 | bytes 17698816 | tf_op jit(solution)/shard_map/cond/branch_1_fun/sub | solution.py:53
  512.9 8.0 %fusion.64 = bf16[512,2,128]{0,2,1:T(8,128)(2,1)S(1)} fusion(f32[512,2,3584]{2,0,1:T(8,128)} %get-tuple-element.414, f32[512,2]{0,1:T(2,128)S(1)} %get-tuple-element.413, bf16[4096,256]{0,1:T(8,128)(2,1)} %copy.114, pred[512]{0:T(512)(128)(4,1)S(1)} %get-tuple-element.398), kind=kOutput, calls=%fused_computation.93 | convolution fusion | flops 947126272 | bytes 15864320 | tf_op jit(solution)/shard_map/cond/branch_1_fun/qhk,kd->qhd/dot_general | solution.py:55
  521.7 3.6 fusion.14
  525.3 10.8 %fusion.316 = (f32[512,2]{0,1:T(2,128)S(1)}, f32[512,2,4096]{2,0,1:T(8,128)}) fusion(pred[512,4096]{1,0:T(8,128)(4,1)} %fusion.14, bf16[4096,256]{1,0:T(8,128)(2,1)S(1)} %get-tuple-element.253, bf16[512,2,128]{2,1,0:T(2,128)(2,1)S(1)} %slice.289), kind=kOutput, calls=%fused_computation.281 | convolution fusion | flops 1090523136 | bytes 20189184 | tf_op jit(solution)/shard_map/cond/branch_1_fun/sub | solution.py:53
  536.1 9.0 %fusion.66 = bf16[512,2,128]{0,2,1:T(8,128)(2,1)S(1)} fusion(f32[512,2,4096]{2,0,1:T(8,128)} %get-tuple-element.416, f32[512,2]{0,1:T(2,128)S(1)} %get-tuple-element.415, bf16[4096,256]{0,1:T(8,128)(2,1)} %copy.114, pred[512]{0:T(512)(128)(4,1)S(1)} %get-tuple-element.397), kind=kOutput, calls=%fused_computation.95 | convolution fusion | flops 1082392576 | bytes 18092544 | tf_op jit(solution)/shard_map/cond/branch_1_fun/qhk,kd->qhd/dot_general | solution.py:55
  546.0 3.3 copy.137
  549.3 37.3 %all_to_all.51 = bf16[32,128,1,256]{3,1,2,0:T(8,128)(2,1)} all-to-all(bf16[32,128,1,256]{3,1,2,0:T(8,128)(2,1)S(1)} %bitcast.282), channel_id=1, replica_groups=mesh['role'=8,'seq'=32] {'seq'}, dimensions={0} | all-to-all | bytes 4194304 | tf_op jit(solution)/shard_map/all_to_all | solution.py:153
  586.6 3.2 copy.138
  (108 shorter events, 49.6 us)
Async XLA Ops:
  8.4 10.2 %copy-start.7 = (s32[4,4]{1,0:T(4,128)S(1)}, s32[4,4]{1,0:T(4,128)}, u32[]{:S(2)}) copy-start(s32[4,4]{1,0:T(4,128)} %param.13) | copy-start | bytes 196
  8.4 10.4 %copy-start.8 = (s32[4,4]{1,0:T(4,128)S(1)}, s32[4,4]{1,0:T(4,128)}, u32[]{:S(2)}) copy-start(s32[4,4]{1,0:T(4,128)} %param.14) | copy-start | bytes 196
  10.0 36.9 %all-to-all-start.1 = ((bf16[128,32,256]{2,0,1:T(8,128)(2,1)}), bf16[128,32,256]{2,0,1:T(8,128)(2,1)S(1)}, u32[]{:S(2)}, u32[]{:S(2)}) async-start(bf16[128,32,256]{2,0,1:T(8,128)(2,1)} %bitcast.280), calls=%async_computation.1 | async-start | bytes 4194304 | tf_op jit(solution)/shard_map/all_to_all | solution.py:126
  46.9 1.3 copy-start
  65.9 8.3 %copy-start.2 = (bf16[1,128,8192]{2,1,0:T(8,128)(2,1)S(1)}, bf16[1,128,8192]{2,1,0:T(8,128)(2,1)}, u32[]{:S(2)}) copy-start(bf16[1,128,8192]{2,1,0:T(8,128)(2,1)} %param.11) | copy-start | bytes 6291460
  65.9 195.4 %all-to-all-start.3 = ((bf16[8,2048,256]{2,1,0:T(8,128)(2,1)}), bf16[8,2048,256]{2,1,0:T(8,128)(2,1)}, u32[]{:S(2)}, u32[]{:S(2)}) async-start(bf16[8,2048,256]{2,1,0:T(8,128)(2,1)} %concatenate.21), calls=%async_computation.3 | async-start | bytes 16777216 | tf_op jit(solution)/shard_map/all_to_all | solution.py:144
  76.7 189.6 %copy-start.5 = (bf16[1,4,4,2048]{3,2,1,0:T(4,128)(2,1)S(1)}, bf16[1,4,4,2048]{3,2,1,0:T(4,128)(2,1)}, u32[]{:S(2)}) copy-start(bf16[1,4,4,2048]{3,2,1,0:T(4,128)(2,1)} %param.16) | copy-start | bytes 196612
  76.7 189.6 %copy-start.6 = (bf16[1,4,4,256]{3,2,1,0:T(4,128)(2,1)S(1)}, bf16[1,4,4,256]{3,2,1,0:T(4,128)(2,1)}, u32[]{:S(2)}) copy-start(bf16[1,4,4,256]{3,2,1,0:T(4,128)(2,1)} %param.15) | copy-start | bytes 24580
  261.3 148.9 %all-to-all-start = ((bf16[128,32,256]{0,2,1:T(8,128)(2,1)}), bf16[128,32,256]{0,2,1:T(8,128)(2,1)}, u32[]{:S(2)}, u32[]{:S(2)}) async-start(bf16[128,32,256]{0,2,1:T(8,128)(2,1)} %bitcast.28), calls=%async_computation | async-start | bytes 4194304 | tf_op jit(solution)/shard_map/all_to_all | solution.py:125
  266.2 326.5 %all-gather.3.cloned.1.call-start = ((), (), s32[]{:S(2)}) async-start(), calls=%async_computation.4 | async-start | bytes 2359296 | tf_op jit(solution)/shard_map/all_gather | solution.py:171
  266.4 148.4 %copy-start.1 = (bf16[128,32,256]{2,0,1:T(8,128)(2,1)S(1)}, bf16[128,32,256]{2,0,1:T(8,128)(2,1)}, u32[]{:S(2)}) copy-start(bf16[128,32,256]{2,0,1:T(8,128)(2,1)} %copy-done) | copy-start | bytes 6291460
  492.5 10.8 %copy-start.4 = (bf16[4,128,1,256]{3,1,0,2:T(8,128)(2,1)S(1)}, bf16[4,128,1,256]{3,1,0,2:T(8,128)(2,1)}, u32[]{:S(2)}) copy-start(bf16[4,128,1,256]{3,1,0,2:T(8,128)(2,1)} %get-tuple-element.382) | copy-start | bytes 786436 | tf_op jit(solution)/shard_map/cond
  512.9 12.4 %copy-start.3 = (bf16[4,128,1,256]{3,1,0,2:T(8,128)(2,1)S(1)}, bf16[4,128,1,256]{3,1,0,2:T(8,128)(2,1)}, u32[]{:S(2)}) copy-start(bf16[4,128,1,256]{3,1,0,2:T(8,128)(2,1)} %get-tuple-element.381) | copy-start | bytes 786436 | tf_op jit(solution)/shard_map/cond
Sparse Core Ops, SparseCore 0:
  410.4 33.2 all-gather.2
where the time goes:
time: 611 us; the launch traced here: 603 us
  waiting for transfers between devices  213 us (35%)
  blocking collectives  181 us (30%)
  matrix products  96.2 us (16%)
  local copies, waits for them, and re-layouts  61.8 us (10%)
  starting transfers between devices  21.8 us (4%)
  other arithmetic  15.1 us (2%)
  between operations  14.4 us (2%)
    all_to_all x1, waiting for transfers between devices, on_device(): lax.all_to_all(outgoing, 'role', split_axis=0, concat_axis=0, tiled=True)  185 us
    psum x1, blocking collectives, on_device(): summed = lax.psum(term_rows, 'seq').astype(jnp.bfloat16)  144 us
    sub x8, matrix products, prefill_attention(): weights = jnp.exp(scores - jnp.max(scores, axis=2, keepdims=True))  51.9 us
    dot_general x8, matrix products, prefill_attention(): jnp.einsum('qhk,kd->qhd', weights, values_all[:row_stop], preferred_eleme...  44.3 us
    all_to_all x1, blocking collectives, on_device(): lax.all_to_all(for_sending(attended.reshape(seq_count, BLOCK, 1, local_he...  37.3 us
    all_to_all x1, waiting for transfers between devices, on_device(): lax.all_to_all(local_cache, 'seq', split_axis=1, concat_axis=0, tiled=True)  27.9 us
    and x8, other arithmetic, prefill_attention(): (segment[row_start:row_stop, None] == segment[None, :row_stop]) & (positi...  14.3 us
  transfers between devices with their start and end apart: 4, of which 2 were waited for; matrix products, arithmetic and copies ran while one was open for 25% of the time, Pallas kernels for 0%

commit v1 on v0

v1 whole, which is shorter than its diff:
```python
import functools

import jax
import jax.numpy as jnp
from jax import lax
from jax.experimental import pallas as pl
from jax.experimental.pallas import tpu as pltpu
from jax.sharding import PartitionSpec as P

MESH = pl.DeviceIdType.MESH
H = 64
KVH = 8
HD = 128
BLOCK = 128
PG = 4
NEG = -1e30
SCALE = HD**-0.5
LOG2E = 1.4426950408889634
SLOTS = 9
HALF = KVH // 2
GROUP = H // KVH
ROWS = 512
KT = 512
WINDOW = 2048


def fused_kernel(
    lengths, serves, q_hbm, kv_hbm, dq, fresh, w_hbm, out_hbm, dec_hbm,
    qbuf, kvbuf, sbuf, sbuf1, peak0, peak1, obuf, zbuf, wbuf, qz, qd, ds, dr, cs, dz, rs_s, rs_r, fz, fo,
    slot_sem, q_sem, own_sem, out_sem, fill_sem, send_sem, din, dout, dlocal
):
    role = lax.axis_index("role")
    seq = lax.axis_index("seq")
    core = seq % 2
    chip = seq // 2
    y = chip % 4
    x = chip // 4
    home = seq // 16
    prefilling = role < PG
    factor = SCALE * LOG2E

    def plane(other):
        return (role, other)

    def line(other):
        return (other, seq)

    def remote(src, dst, send, recv, device):
        return pltpu.make_async_remote_copy(
            src_ref=src, dst_ref=dst, send_sem=send, recv_sem=recv, device_id=device, device_id_type=MESH)

    def await_bytes(ref, sem):
        pltpu.make_async_copy(ref, ref, sem).wait()

    def q_columns(half, h):
        return q_hbm.at[:, pl.ds(pl.multiple_of((half * 32 + h) * HD, HD), HD)]

    def kv_columns(half, j):
        return kv_hbm.at[:, pl.ds(pl.multiple_of(half * HALF * 256 + j * 256, 256), 256)]

    def chunk(slot, j):
        return kvbuf.at[j, pl.ds(pl.multiple_of((8 - slot) * 256, 256), 256), :]

    def own_rows(j):
        return kvbuf.at[j, pl.ds(pl.multiple_of(2048 + core * 128, 128), 128), :]

    barrier = pltpu.get_barrier_semaphore()

    def greet(d, carry):
        pl.semaphore_signal(barrier, inc=1, device_id=plane((seq + d) % 32), device_id_type=MESH)
        return carry

    lax.fori_loop(1, 32, greet, 0)

    @pl.when(prefilling)
    def _():
        for g in range(PG):
            pl.semaphore_signal(barrier, inc=1, device_id=line(PG + g), device_id_type=MESH)
        for j in range(HALF):
            pltpu.make_async_copy(kv_columns(core, j), own_rows(j), own_sem.at[j]).start()

        def keep_q(h, carry):
            pltpu.make_async_copy(q_columns(core, h), qbuf.at[core, h], q_sem.at[1]).start()
            return carry

        lax.fori_loop(0, 32, keep_q, 0)
        pl.semaphore_wait(barrier, 35)

    @pl.when(role >= PG)
    def _():
        for d in range(1, 2 * PG):
            pl.semaphore_signal(barrier, inc=1, device_id=line((role + d) % (2 * PG)), device_id_type=MESH)
        pltpu.make_async_copy(w_hbm, wbuf, dlocal.at[0]).start()
        zbuf[...] = jnp.zeros_like(zbuf)
        for i in range(8):
            pltpu.make_async_copy(zbuf, out_hbm.at[:, i * 1024:(i + 1) * 1024], fill_sem.at[i]).start()
        pl.semaphore_wait(barrier, 38)

    def dec_columns(s):
        return dec_hbm.at[:, pl.ds(pl.multiple_of(s * 256, 256), 256)]

    sibling = plane(seq + 1 - 2 * core)

    def finish_own():
        await_first = prefilling

        @pl.when(await_first)
        def _():
            await_bytes(fz.at[0:4], din.at[5])

        @pl.when(jnp.logical_not(await_first))
        def _():
            await_bytes(fz.at[0:3], din.at[5])

        to = lax.broadcasted_iota(jnp.int32, (64, 64), 0)
        at = lax.broadcasted_iota(jnp.int32, (64, 64), 1)
        order = (at == ((to // 4) % 4) * 16 + (to % 4) * 4 + to // 16).astype(jnp.bfloat16)
        slab = jnp.dot(order, fz[0:4].reshape(64, 256), preferred_element_type=jnp.float32)
        fo[...] = slab.astype(jnp.bfloat16)
        pltpu.make_async_copy(fo, dec_columns(seq), dlocal.at[1]).start()

        def spread(d, carry):
            other = ((chip + d) % 16) * 2 + core
            remote(fo, dec_columns(seq), dout.at[6], din.at[6], plane(other)).start()
            return carry

        lax.fori_loop(1, 16, spread, 0)

    def finish_pair():
        pltpu.make_async_copy(fo, dec_columns(seq), dlocal.at[1]).wait()
        await_bytes(dec_hbm.at[:, 0:3840], din.at[6])

        def mirror(c, carry):
            remote(dec_columns(2 * c + core), dec_columns(2 * c + core), dout.at[7], din.at[7], sibling).start()
            return carry

        lax.fori_loop(0, 16, mirror, 0)

    def finish_wait():
        await_bytes(dec_hbm.at[:, 0:3840], dout.at[6])
        await_bytes(dec_hbm.at[:, 0:4096], dout.at[7])
        await_bytes(dec_hbm.at[:, 0:4096], din.at[7])

    @pl.when(prefilling)
    def _():
        right, left = (y + 1) % 4, (y + 3) % 4

        def device(xx, yy):
            return plane((xx * 4 + yy) * 2 + core)

        for j in range(HALF):
            remote(kv_columns(1 - core, j), own_rows(j), send_sem.at[10], slot_sem.at[0, j], sibling).start()

        for slot in range(1, SLOTS):
            @pl.when(chip < slot)
            def _(slot=slot):
                for j in range(HALF):
                    kvbuf[j, (8 - slot) * 256:(9 - slot) * 256, :] = jnp.zeros((256, 256), jnp.bfloat16)

        def wait_slot(slot, j):
            @pl.when(chip >= slot)
            def _():
                await_bytes(chunk(slot, j), slot_sem.at[slot, j])

        def send(kind, src, dst, j, xx, yy):
            remote(chunk(src, j), chunk(dst, j), send_sem.at[kind], slot_sem.at[dst, j], device(xx, yy)).start()

        def own(j):
            pltpu.make_async_copy(kv_columns(core, j), own_rows(j), own_sem.at[j]).wait()
            await_bytes(own_rows(j), slot_sem.at[0, j])

            @pl.when(x < 3)
            def _():
                send(0, 0, 4, j, (x + 1) % 4, y)

            @pl.when(x < 2)
            def _():
                send(1, 0, 8, j, (x + 2) % 4, y)

        def own_along_y(j):
            @pl.when(y < 3)
            def _():
                send(2, 0, 1, j, x, right)

            @pl.when(y == 0)
            def _():
                send(3, 0, 3, j, x, left)

        right_dst = jnp.where(y < 3, 5, 1)
        left_dst = jnp.where(y > 0, 3, 7)
        right_fwd = jnp.where(y < 3, 1, 5)
        left_fwd = jnp.where(y > 0, 7, 3)

        def inject(j):
            wait_slot(4, j)

            @pl.when(x >= 1)
            def _():
                send(4, 4, right_dst, j, x, right)
                send(5, 4, left_dst, j, x, left)

            wait_slot(8, j)

            @pl.when(jnp.logical_and(x >= 2, y == 3))
            def _():
                send(6, 8, 5, j, x, right)

            @pl.when(jnp.logical_and(x >= 2, y > 0))
            def _():
                send(7, 8, 7, j, x, left)

        def forward(j):
            wait_slot(right_fwd, j)

            @pl.when(chip >= right_fwd)
            def _():
                send(8, right_fwd, 2, j, x, right)

            wait_slot(left_fwd, j)

            @pl.when(chip >= left_fwd)
            def _():
                send(9, left_fwd, 6, j, x, left)

        def rest(j):
            wait_slot(6 - right_fwd, j)
            wait_slot(10 - left_fwd, j)
            wait_slot(2, j)
            wait_slot(6, j)

        counts = [lengths[role, i] for i in range(4)]
        served = [serves[role, i] for i in range(4)]
        blocks = [(n + 127) // 128 for n in counts]
        starts = [0, blocks[0], blocks[0] + blocks[1], blocks[0] + blocks[1] + blocks[2]]

        def pick(block, values):
            chosen = values[0]
            for i in range(1, 4):
                chosen = jnp.where(block >= starts[i], values[i], chosen)
            return chosen

        firsts, lives = [], []
        for e in range(2):
            block = 2 * chip + e
            first = pick(block, starts)
            firsts.append((first - (2 * chip - 15 + e)) * 128)
            lives.append(pick(block, counts) - (block - first) * 128)

        at_home = home == core

        def spread_queries():
            await_bytes(qz, din.at[0])

            @pl.when(at_home)
            def _():
                qd[seq % 16] = qz[...]

            def one(d, carry):
                other = ((chip + d) % 16) * 2 + home

                @pl.when(other != seq)
                def _():
                    remote(qz, qd.at[seq % 16], dout.at[1], din.at[1], plane(other)).start()

                return carry

            lax.fori_loop(0, 16, one, 0)

        def await_many(buffer, sem):
            @pl.when(at_home)
            def _():
                await_bytes(buffer.at[0:15], sem)

            @pl.when(jnp.logical_not(at_home))
            def _():
                await_bytes(buffer, sem)

        lanes = lax.broadcasted_iota(jnp.int32, (32, HD), 1)

        def partial_terms():
            await_many(qd, din.at[1])
            for e in range(2):
                group = pick(2 * chip + e, served)
                live = lives[e]

                for j in range(HALF):
                    q = jnp.zeros((4, 8, HD), jnp.float32)
                    for g in range(PG):
                        q = jnp.where(group == g, qd[4 * j:4 * j + 4, g], q)
                    q = q.reshape(32, HD).astype(jnp.bfloat16)
                    keys = kvbuf[j, 2048 + 128 * e:2176 + 128 * e, 0:HD]
                    values = kvbuf[j, 2048 + 128 * e:2176 + 128 * e, HD:2 * HD]
                    s = lax.dot_general(q, keys, (((1,), (1,)), ((), ())), preferred_element_type=jnp.float32)
                    s = jnp.where(lanes < live, s, NEG)
                    m = jnp.max(s, axis=1, keepdims=True)
                    w = jnp.exp2((s - m) * factor)
                    total = jnp.sum(w, axis=1, keepdims=True)
                    o = jnp.dot(w.astype(jnp.bfloat16), values, preferred_element_type=jnp.float32)
                    ds[4 * j:4 * j + 4, e, 0] = o.reshape(4, 8, HD)
                    ds[4 * j:4 * j + 4, e, 1] = jnp.where(lanes < 64, m, total).reshape(4, 8, HD)

            @pl.when(at_home)
            def _():
                dr[chip] = ds[seq % 16]

            def out(d, carry):
                other = 16 * core + (chip + d) % 16

                @pl.when(other != seq)
                def _():
                    remote(ds.at[(chip + d) % 16], dr.at[chip], dout.at[2], din.at[2], plane(other)).start()

                return carry

            lax.fori_loop(0, 16, out, 0)

        which = lax.broadcasted_iota(jnp.int32, (PG, 8, HD), 0)

        def combine_terms():
            await_many(dr, din.at[2])

            terms = []
            top = jnp.full((PG, 8, HD), NEG, jnp.float32)
            for b in range(32):
                flag = which == pick(jnp.int32(b), served)
                m = jnp.broadcast_to(dr[b // 2, b % 2, 1][:, 0:1], (8, HD))[None]
                top = jnp.maximum(top, jnp.where(flag, m, NEG))
                terms.append((flag, m))
            total = jnp.zeros((PG, 8, HD), jnp.float32)
            mixed = jnp.zeros((PG, 8, HD), jnp.float32)
            for b in range(32):
                flag, m = terms[b]
                part = jnp.broadcast_to(dr[b // 2, b % 2, 1][:, 64:65], (8, HD))[None]
                add = jnp.where(flag, jnp.exp2((jnp.minimum(m, top) - top) * factor), 0.0)
                total = total + add * part
                mixed = mixed + add * dr[b // 2, b % 2, 0][None]
            lane3 = lax.broadcasted_iota(jnp.int32, (PG, 8, HD), 2)
            cs[:, 0] = mixed
            cs[:, 1] = jnp.where(lane3 < 64, top, total)
            for g in range(PG):
                remote(cs.at[g], dz.at[role], dout.at[3], din.at[3], line(PG + g)).start()

        for j in range(HALF):
            own(j)
            if j < 2:
                own_along_y(j)

        spread_queries()

        def start_q(h, carry):
            remote(q_columns(1 - core, h), qbuf.at[core, h], send_sem.at[11], q_sem.at[0], sibling).start()
            return carry

        lax.fori_loop(0, 32, start_q, 0)
        partial_terms()
        inject(0)
        own_along_y(2)
        forward(0)
        combine_terms()
        inject(1)
        own_along_y(3)
        rest(0)

        await_bytes(qbuf.at[0], q_sem.at[0])
        await_bytes(qbuf.at[0], q_sem.at[1])

        lane = lax.broadcasted_iota(jnp.int32, (1, KT), 1)
        tri = lax.broadcasted_iota(jnp.int32, (ROWS, 128), 0) % 128 >= lax.broadcasted_iota(jnp.int32, (ROWS, 128), 1)
        row_in = lax.broadcasted_iota(jnp.int32, (ROWS, 128), 0) % 128
        ones = jnp.ones((KT, HD), jnp.bfloat16)
        last = WINDOW // KT - 1

        def place(n):
            j, u = n // 4, n % 4
            return j, u // 2, j * GROUP + (u % 2) * 4

        def key_rows(j, e, kt):
            return j, pl.ds(pl.multiple_of(128 + e * 128 + kt * KT, 128), KT)

        def weave(current, following):
            if following is not None:
                n, scores, peaks = following
                j, e, base = place(n)
                threshold = jnp.where(e == 0, firsts[0], firsts[1])
                q = qbuf[e, pl.ds(base, 4)].reshape(ROWS, HD)
                peak = None
            if current is not None:
                cn, cscores, cpeaks = current
                cj, ce, cbase = place(cn)
                total = None
            for kt in range(WINDOW // KT):
                if following is not None:
                    rows = key_rows(j, e, kt)
                    s = lax.dot_general(
                        q, kvbuf[rows[0], rows[1], 0:HD], (((1,), (1,)), ((), ())), preferred_element_type=jnp.float32)
                if current is not None:
                    weights = [
                        jnp.exp2((cscores[:, kt * KT + i * 128:kt * KT + (i + 1) * 128] - cpeaks[...]) * factor)
                        for i in range(KT // 128)
                    ]
                    rows = key_rows(cj, ce, kt)
                    product = jnp.dot(
                        jnp.concatenate(weights, axis=1).astype(jnp.bfloat16),
                        jnp.concatenate([kvbuf[rows[0], rows[1], HD:2 * HD], ones], axis=1),
                        preferred_element_type=jnp.float32)
                    total = product if total is None else total + product
                if following is not None:
                    s = s + jnp.where(lane + kt * KT >= threshold, 0.0, NEG)
                    pieces = [s[:, i * 128:(i + 1) * 128] for i in range(KT // 128)]
                    if kt == last:
                        pieces[-1] = jnp.where(tri, pieces[-1], NEG)
                    for i, piece in enumerate(pieces):
                        scores[:, kt * KT + i * 128:kt * KT + (i + 1) * 128] = piece
                    while len(pieces) > 1:
                        pieces = [jnp.maximum(a, b) for a, b in zip(pieces[::2], pieces[1::2])]
                    peak = pieces[0] if peak is None else jnp.maximum(peak, pieces[0])
            if following is not None:
                peaks[...] = jnp.broadcast_to(jnp.max(peak, axis=1, keepdims=True), (ROWS, 128))
            if current is not None:
                live = jnp.where(ce == 0, lives[0], lives[1])
                mixed = total[:, :HD] / total[:, HD:]
                mixed = jnp.where(row_in < live, mixed, 0.0).astype(jnp.bfloat16)
                obuf[ce, pl.ds(cbase, 4)] = mixed.reshape(4, BLOCK, HD)
                for i in range(4):
                    columns = out_hbm.at[:, pl.ds(pl.multiple_of((core * 32 + cbase + i) * HD, HD), HD)]

                    @pl.when(ce == core)
                    def _(i=i, columns=columns):
                        pltpu.make_async_copy(obuf.at[ce, cbase + i], columns, out_sem.at[0]).start()

                    @pl.when(ce != core)
                    def _(i=i, columns=columns):
                        remote(obuf.at[ce, cbase + i], columns, send_sem.at[12], out_sem.at[1], sibling).start()

        weave(None, (jnp.int32(0), sbuf, peak0))

        def pair(i, carry):
            j = i // 2
            weave((2 * i, sbuf, peak0), (2 * i + 1, sbuf1, peak1))

            @pl.when(jnp.logical_and(i % 2 == 0, j < HALF - 1))
            def _():
                forward(j + 1)

            @pl.when(jnp.logical_and(i % 2 == 1, j < HALF - 2))
            def _():
                inject(j + 2)

            @pl.when(jnp.logical_and(i % 2 == 1, j < HALF - 1))
            def _():
                rest(j + 1)

            @pl.when(i == 6)
            def _():
                finish_own()

            weave((2 * i + 1, sbuf1, peak1), (2 * i + 2, sbuf, peak0))
            return carry

        lax.fori_loop(0, 7, pair, 0)
        weave((jnp.int32(14), sbuf, peak0), (jnp.int32(15), sbuf1, peak1))
        finish_pair()
        weave((jnp.int32(15), sbuf1, peak1), None)

        span = kvbuf.at[:, 0:256, :]

        def sent(kind, condition):
            @pl.when(condition)
            def _():
                await_bytes(span, send_sem.at[kind])

        sent(0, x < 3)
        sent(1, x < 2)
        sent(2, y < 3)
        sent(3, y == 0)
        sent(4, x >= 1)
        sent(5, x >= 1)
        sent(6, jnp.logical_and(x >= 2, y == 3))
        sent(7, jnp.logical_and(x >= 2, y > 0))
        sent(8, chip >= right_fwd)
        sent(9, chip >= left_fwd)
        await_bytes(kvbuf.at[:, 0:128, :], send_sem.at[10])
        await_bytes(qbuf.at[0], send_sem.at[11])
        await_bytes(obuf.at[0], send_sem.at[12])
        await_bytes(obuf.at[0], out_sem.at[0])
        await_many(qd, dout.at[1])
        await_many(dr, dout.at[2])
        await_bytes(cs, dout.at[3])
        await_bytes(obuf.at[0], out_sem.at[1])
        finish_wait()

    @pl.when(role >= PG)
    def _():
        group = role - PG
        for p in range(PG):
            remote(dq.at[p], qz.at[group], dout.at[0], din.at[0], line(p)).start()
        pltpu.make_async_copy(w_hbm, wbuf, dlocal.at[0]).wait()
        await_bytes(dz, din.at[3])
        step = lax.broadcasted_iota(jnp.int32, (8, HD), 0) % 4
        tiles = []
        for p in range(PG):
            pair = dz[p, 1]
            m = jnp.broadcast_to(pair[:, 0:1], (8, HD))
            part = jnp.broadcast_to(pair[:, 64:65], (8, HD))
            q = dq[p]
            scores = []
            for t in range(4):
                s = jnp.sum(q * fresh[p, 0, t:t + 1, :], axis=1, keepdims=True)
                scores.append(jnp.where(step >= t, jnp.broadcast_to(s, (8, HD)), NEG))
            top = m
            for s in scores:
                top = jnp.maximum(top, s)
            old = jnp.exp2((m - top) * factor)
            total = part * old
            mixed = dz[p, 0] * old
            for t in range(4):
                w = jnp.exp2((scores[t] - top) * factor)
                total = total + w
                mixed = mixed + w * fresh[p, 1, t:t + 1, :]
            tiles.append(mixed / total)
        rows = jnp.concatenate(tiles, axis=0).astype(jnp.bfloat16)
        to = lax.broadcasted_iota(jnp.int32, (16, 32), 0)
        at = lax.broadcasted_iota(jnp.int32, (16, 32), 1)
        halves = []
        for h in range(2):
            chosen = (at == (to // 4) * 8 + h * 4 + to % 4).astype(jnp.bfloat16)
            halves.append(jnp.dot(chosen, rows, preferred_element_type=jnp.float32).astype(jnp.bfloat16))
        attended = jnp.concatenate(halves, axis=1)

        def project(i, carry):
            others = [(seq + 4 * i + d) % 32 for d in range(4)]
            for other in others:
                columns = pl.ds(pl.multiple_of(other * 256, 256), 256)
                rs_s[other] = jnp.dot(attended, wbuf[:, columns], preferred_element_type=jnp.float32)
            for other in others:
                @pl.when(other != seq)
                def _(other=other):
                    remote(rs_s.at[other], rs_r.at[seq], dout.at[4], din.at[4], plane(other)).start()

            return carry

        lax.fori_loop(0, 8, project, 0)
        rs_r[seq] = rs_s[seq]
        await_bytes(rs_r.at[0:31], din.at[4])

        def add(i, total):
            four = [rs_r[4 * i + d] for d in range(4)]
            return total + ((four[0] + four[1]) + (four[2] + four[3]))

        summed = lax.fori_loop(0, 8, add, jnp.zeros((16, 256), jnp.float32))
        fz[group] = summed.astype(jnp.bfloat16)
        for d in range(1, 2 * PG):
            remote(fz.at[group], fz.at[group], dout.at[5], din.at[5], line((role + d) % (2 * PG))).start()
        finish_own()
        finish_pair()
        await_bytes(qz, dout.at[0])
        await_bytes(rs_s.at[0:31], dout.at[4])
        await_bytes(fz.at[0:7], dout.at[5])
        for i in range(8):
            pltpu.make_async_copy(zbuf, out_hbm.at[:, i * 1024:(i + 1) * 1024], fill_sem.at[i]).wait()
        finish_wait()


def fused(prompt_lengths, decode_group, queries, kv, dq, fresh, out_weight):
    smem = pl.BlockSpec(memory_space=pltpu.SMEM)
    vmem = pl.BlockSpec(memory_space=pltpu.VMEM)
    hbm = pl.BlockSpec(memory_space=pl.ANY)
    return pl.pallas_call(
        fused_kernel,
        out_shape=[
            jax.ShapeDtypeStruct((BLOCK, H * HD), jnp.bfloat16),
            jax.ShapeDtypeStruct((64, H * HD), jnp.bfloat16),
        ],
        in_specs=[smem, smem, hbm, hbm, vmem, vmem, hbm],
        out_specs=[hbm, hbm],
        scratch_shapes=[
            pltpu.VMEM((2, 32, BLOCK, HD), jnp.bfloat16),
            pltpu.VMEM((HALF, SLOTS * 256, 256), jnp.bfloat16),
            pltpu.VMEM((ROWS, WINDOW), jnp.float32),
            pltpu.VMEM((ROWS, WINDOW), jnp.float32),
            pltpu.VMEM((ROWS, 128), jnp.float32),
            pltpu.VMEM((ROWS, 128), jnp.float32),
            pltpu.VMEM((2, 32, BLOCK, HD), jnp.bfloat16),
            pltpu.VMEM((BLOCK, 1024), jnp.bfloat16),
            pltpu.VMEM((256, 8192), jnp.bfloat16),
            pltpu.VMEM((PG, 8, HD), jnp.float32),
            pltpu.VMEM((16, PG, 8, HD), jnp.float32),
            pltpu.VMEM((16, 2, 2, 8, HD), jnp.float32),
            pltpu.VMEM((16, 2, 2, 8, HD), jnp.float32),
            pltpu.VMEM((PG, 2, 8, HD), jnp.float32),
            pltpu.VMEM((PG, 2, 8, HD), jnp.float32),
            pltpu.VMEM((32, 16, 256), jnp.float32),
            pltpu.VMEM((32, 16, 256), jnp.float32),
            pltpu.VMEM((8, 16, 256), jnp.bfloat16),
            pltpu.VMEM((64, 256), jnp.bfloat16),
            pltpu.SemaphoreType.DMA((SLOTS, HALF)),
            pltpu.SemaphoreType.DMA((2,)),
            pltpu.SemaphoreType.DMA((HALF,)),
            pltpu.SemaphoreType.DMA((2,)),
            pltpu.SemaphoreType.DMA((8,)),
            pltpu.SemaphoreType.DMA((13,)),
            pltpu.SemaphoreType.DMA((8,)),
            pltpu.SemaphoreType.DMA((8,)),
            pltpu.SemaphoreType.DMA((2,)),
        ],
        compiler_params=pltpu.CompilerParams(
            collective_id=0, has_side_effects=True, vmem_limit_bytes=62 * 1024 * 1024
        ),
        cost_estimate=pl.CostEstimate(flops=17_000_000_000, bytes_accessed=16_000_000, transcendentals=17_000_000),
    )(prompt_lengths, decode_group, queries, kv, dq, fresh, out_weight)


def on_device(prefill_queries, prefill_kv, prompt_lengths, decode_group, decode_queries, decode_kv, out_weight):
    kv_head = lax.axis_index("seq") // (lax.axis_size("seq") // KVH)
    dq = decode_queries[0].reshape(4, PG, 2, HD).transpose(1, 2, 0, 3).reshape(PG, 8, HD).astype(jnp.float32)
    fresh = lax.dynamic_slice_in_dim(decode_kv[0], kv_head * 2 * HD, 2 * HD, 2)
    fresh = fresh.reshape(4, PG, 2, HD).transpose(1, 2, 0, 3).astype(jnp.float32)
    prefill_out, decode_out = fused(
        prompt_lengths, decode_group, prefill_queries[0], prefill_kv[0], dq, fresh, out_weight
    )
    return prefill_out[None], decode_out.reshape(4, PG, PG, -1)


def solution(mesh):
    in_specs = (
        P("role", "seq", None),
        P("role", "seq", None),
        P(),
        P(),
        P("role", None, None, "seq"),
        P("role", None, None, None),
        P("seq", None),
    )
    out_specs = (P("role", "seq", None), P())
    return jax.shard_map(on_device, mesh=mesh, in_specs=in_specs, out_specs=out_specs, check_vma=False)
```

time: 611 us -> 105 us (0.17); the launches traced: 603 us -> 104 us
  waiting for transfers between devices: 213 us -> 0 us
  blocking collectives: 181 us -> 0 us
  Pallas kernels: 0 us -> 97.4 us
  matrix products: 96.2 us -> 0 us
  local copies, waits for them, and re-layouts: 61.8 us -> 5.64 us
  starting transfers between devices: 21.8 us -> 0 us
  other arithmetic: 15.1 us -> 0.71 us
  between operations: 14.4 us -> 0.67 us
    all_to_all x3 -> x0, waiting for transfers between devices: 213 us -> none  [the longest x1 185 us: on_device(): lax.all_to_all(outgoing, 'role', split_axis=0, concat_axis=0, tiled=True)]
    psum x1 -> x0, blocking collectives: 144 us -> none  [on_device(): summed = lax.psum(term_rows, 'seq').astype(jnp.bfloat16)]
    pallas_call x0 -> x1, Pallas kernels: none -> 97.4 us  [fused(): pl.pallas_call(fused_kernel, out_shape=[jax.ShapeDtypeStruct((BLOCK, H *...]
    sub x8 -> x0, matrix products: 51.9 us -> none  [prefill_attention(): weights = jnp.exp(scores - jnp.max(scores, axis=2, keepdims=True))]
    dot_general x8 -> x0, matrix products: 44.3 us -> none  [prefill_attention(): jnp.einsum('qhk,kd->qhd', weights, values_all[:row_stop], preferred_eleme...]
    all_to_all x1 -> x0, blocking collectives: 37.3 us -> none  [on_device(): lax.all_to_all(for_sending(attended.reshape(seq_count, BLOCK, 1, local_he...]
    all_to_all x3 -> x0, starting transfers between devices: 21.8 us -> none  [the longest x1 8.59 us: on_device(): lax.all_to_all(local_cache, 'seq', split_axis=1, concat_axis=0, tiled=True)]
    and x8 -> x0, other arithmetic: 14.3 us -> none  [prefill_attention(): (segment[row_start:row_stop, None] == segment[None, :row_stop]) & (positi...]
  transfers between devices with their start and end apart: 4 -> 0, of which waited for: 2 -> 0; matrix products, arithmetic and copies ran while one was open for 25% -> 0% of each run, Pallas kernels for 0% -> 0%
where the time goes in v1:
time: 105 us; the launch traced here: 104 us
  Pallas kernels  97.4 us (93%)
  local copies, waits for them, and re-layouts  5.64 us (5%)
    pallas_call x1, Pallas kernels, fused(): pl.pallas_call(fused_kernel, out_shape=[jax.ShapeDtypeStruct((BLOCK, H *...  97.4 us
    reshape x1, local copies, waits for them, and re-layouts, on_device(): return (prefill_out[None], decode_out.reshape(4, PG, PG, -1))  2.39 us

profile of v1, /device:TPU:1, one launch (start us, length us, event | category | flops | bytes accessed | tf_op | source)
XLA Modules:
  0.0 104.4 jit_solution(5727386874043181420)
XLA Ops:
  0.6 0.7 bitcast_convert_fusion
  1.4 0.6 copy.13
  2.0 0.7 reshape.20
  2.7 0.6 copy.10
  3.3 97.4 %shard_map.86 = (bf16[128,8192]{1,0:T(8,128)(2,1)}, bf16[64,8192]{1,0:T(8,128)(2,1)}) custom-call(s32[4,4]{1,0:T(4,128)} %lengths.1, s32[4,4]{1,0:T(4,128)} %serves.1, bf16[128,8192]{1,0:T(8,128)(2,1)} %bitcast.15, bf16[128,2048]{1,0:T(8,128)(2,1)} %bitcast.16, f32[4,8,128]{2,1,0:T(8,128)} %bitcast.14, f32[4,2,4,128]{3,2,1,0:T(4,128)} %bitcast.13, ...), custom_call_target="tpu_custom_call" | custom-call | flops 16999999488 | bytes 16000000 | tf_op jit(solution)/shard_map/pallas_call | solution.py:568
  100.7 0.0 copy-start
  100.7 2.4 %reshape.17 = bf16[4,4,4,8192]{3,2,1,0:T(4,128)(2,1)} reshape(bf16[64,8192]{1,0:T(8,128)(2,1)} %get-tuple-element.5) | data formatting | bytes 2097152 | tf_op jit(solution)/shard_map/reshape | solution.py:621
  103.1 0.0 copy-done
  103.1 1.3 %copy.15 = bf16[1,128,8192]{2,1,0:T(8,128)(2,1)} copy(bf16[1,128,8192]{2,1,0:T(8,128)(2,1)S(1)} %bitcast.12) | data formatting | bytes 4194304
Async XLA Ops:
  100.7 2.4 %copy-start = (bf16[128,8192]{1,0:T(8,128)(2,1)S(1)}, bf16[128,8192]{1,0:T(8,128)(2,1)}, u32[]{:S(2)}) copy-start(bf16[128,8192]{1,0:T(8,128)(2,1)} %get-tuple-element.4) | copy-start | bytes 6291460

commit v2 on v1

--- a/solution.py
+++ b/solution.py
@@ -26,7 +26,7 @@
 
 def fused_kernel(
     lengths, serves, q_hbm, kv_hbm, dq, fresh, w_hbm, out_hbm, dec_hbm,
-    qbuf, kvbuf, sbuf, sbuf1, peak0, peak1, obuf, zbuf, wbuf, qz, qd, ds, dr, cs, dz, rs_s, rs_r, fz, fo,
+    qbuf, kvbuf, sbuf, sbuf1, peak0, peak1, obuf, zbuf, wbuf, qz, qb, qd, ds, dr, cs, dz, rs_s, rs_r, fz, fo,
     slot_sem, q_sem, own_sem, out_sem, fill_sem, send_sem, din, dout, dlocal
 ):
     role = lax.axis_index("role")
@@ -96,8 +96,7 @@
             pltpu.make_async_copy(zbuf, out_hbm.at[:, i * 1024:(i + 1) * 1024], fill_sem.at[i]).start()
         pl.semaphore_wait(barrier, 38)
 
-    def dec_columns(s):
-        return dec_hbm.at[:, pl.ds(pl.multiple_of(s * 256, 256), 256)]
+    mine = dec_hbm.at[chip, core]
 
     sibling = plane(seq + 1 - 2 * core)
 
@@ -117,29 +116,24 @@
         order = (at == ((to // 4) % 4) * 16 + (to % 4) * 4 + to // 16).astype(jnp.bfloat16)
         slab = jnp.dot(order, fz[0:4].reshape(64, 256), preferred_element_type=jnp.float32)
         fo[...] = slab.astype(jnp.bfloat16)
-        pltpu.make_async_copy(fo, dec_columns(seq), dlocal.at[1]).start()
+        pltpu.make_async_copy(fo, mine, dlocal.at[1]).start()
 
         def spread(d, carry):
             other = ((chip + d) % 16) * 2 + core
-            remote(fo, dec_columns(seq), dout.at[6], din.at[6], plane(other)).start()
+            remote(fo, mine, dout.at[6], din.at[6], plane(other)).start()
             return carry
 
         lax.fori_loop(1, 16, spread, 0)
 
     def finish_pair():
-        pltpu.make_async_copy(fo, dec_columns(seq), dlocal.at[1]).wait()
-        await_bytes(dec_hbm.at[:, 0:3840], din.at[6])
-
-        def mirror(c, carry):
-            remote(dec_columns(2 * c + core), dec_columns(2 * c + core), dout.at[7], din.at[7], sibling).start()
-            return carry
-
-        lax.fori_loop(0, 16, mirror, 0)
+        pltpu.make_async_copy(fo, mine, dlocal.at[1]).wait()
+        await_bytes(dec_hbm.at[0:15, 0], din.at[6])
+        remote(dec_hbm.at[:, core], dec_hbm.at[:, core], dout.at[7], din.at[7], sibling).start()
 
     def finish_wait():
-        await_bytes(dec_hbm.at[:, 0:3840], dout.at[6])
-        await_bytes(dec_hbm.at[:, 0:4096], dout.at[7])
-        await_bytes(dec_hbm.at[:, 0:4096], din.at[7])
+        await_bytes(dec_hbm.at[0:15, 0], dout.at[6])
+        await_bytes(dec_hbm.at[:, 0], dout.at[7])
+        await_bytes(dec_hbm.at[:, 0], din.at[7])
 
     @pl.when(prefilling)
     def _():
@@ -151,12 +145,6 @@
         for j in range(HALF):
             remote(kv_columns(1 - core, j), own_rows(j), send_sem.at[10], slot_sem.at[0, j], sibling).start()
 
-        for slot in range(1, SLOTS):
-            @pl.when(chip < slot)
-            def _(slot=slot):
-                for j in range(HALF):
-                    kvbuf[j, (8 - slot) * 256:(9 - slot) * 256, :] = jnp.zeros((256, 256), jnp.bfloat16)
-
         def wait_slot(slot, j):
             @pl.when(chip >= slot)
             def _():
@@ -165,10 +153,11 @@
         def send(kind, src, dst, j, xx, yy):
             remote(chunk(src, j), chunk(dst, j), send_sem.at[kind], slot_sem.at[dst, j], device(xx, yy)).start()
 
-        def own(j):
+        def own_wait(j):
             pltpu.make_async_copy(kv_columns(core, j), own_rows(j), own_sem.at[j]).wait()
             await_bytes(own_rows(j), slot_sem.at[0, j])
 
+        def own(j):
             @pl.when(x < 3)
             def _():
                 send(0, 0, 4, j, (x + 1) % 4, y)
@@ -250,17 +239,18 @@
 
         def spread_queries():
             await_bytes(qz, din.at[0])
+            qb[...] = qz[...].reshape(32, HD).astype(jnp.bfloat16)
 
             @pl.when(at_home)
             def _():
-                qd[seq % 16] = qz[...]
+                qd[seq % 16] = qb[...]
 
             def one(d, carry):
                 other = ((chip + d) % 16) * 2 + home
 
                 @pl.when(other != seq)
                 def _():
-                    remote(qz, qd.at[seq % 16], dout.at[1], din.at[1], plane(other)).start()
+                    remote(qb, qd.at[seq % 16], dout.at[1], din.at[1], plane(other)).start()
 
                 return carry
 
@@ -279,14 +269,16 @@
 
         def partial_terms():
             await_many(qd, din.at[1])
+            stats = []
             for e in range(2):
                 group = pick(2 * chip + e, served)
                 live = lives[e]
 
                 for j in range(HALF):
                     q = jnp.zeros((4, 8, HD), jnp.float32)
+                    wide = qd[4 * j:4 * j + 4].astype(jnp.float32).reshape(4, PG, 8, HD)
                     for g in range(PG):
-                        q = jnp.where(group == g, qd[4 * j:4 * j + 4, g], q)
+                        q = jnp.where(group == g, wide[:, g], q)
                     q = q.reshape(32, HD).astype(jnp.bfloat16)
                     keys = kvbuf[j, 2048 + 128 * e:2176 + 128 * e, 0:HD]
                     values = kvbuf[j, 2048 + 128 * e:2176 + 128 * e, HD:2 * HD]
@@ -296,8 +288,13 @@
                     w = jnp.exp2((s - m) * factor)
                     total = jnp.sum(w, axis=1, keepdims=True)
                     o = jnp.dot(w.astype(jnp.bfloat16), values, preferred_element_type=jnp.float32)
-                    ds[4 * j:4 * j + 4, e, 0] = o.reshape(4, 8, HD)
-                    ds[4 * j:4 * j + 4, e, 1] = jnp.where(lanes < 64, m, total).reshape(4, 8, HD)
+                    ds[4 * j:4 * j + 4, e] = o.reshape(4, 8, HD)
+                    stat = jnp.where(lanes < 64, m, total)
+                    if e == 0:
+                        stats.append(stat)
+                    else:
+                        stat = jnp.where(lanes % 64 < 32, stats[j], stat)
+                        ds[4 * j:4 * j + 4, 2] = stat.reshape(4, 8, HD)
 
             @pl.when(at_home)
             def _():
@@ -323,42 +320,51 @@
             top = jnp.full((PG, 8, HD), NEG, jnp.float32)
             for b in range(32):
                 flag = which == pick(jnp.int32(b), served)
-                m = jnp.broadcast_to(dr[b // 2, b % 2, 1][:, 0:1], (8, HD))[None]
+                m = jnp.broadcast_to(dr[b // 2, 2][:, 32 * (b % 2):32 * (b % 2) + 1], (8, HD))[None]
                 top = jnp.maximum(top, jnp.where(flag, m, NEG))
                 terms.append((flag, m))
             total = jnp.zeros((PG, 8, HD), jnp.float32)
             mixed = jnp.zeros((PG, 8, HD), jnp.float32)
             for b in range(32):
                 flag, m = terms[b]
-                part = jnp.broadcast_to(dr[b // 2, b % 2, 1][:, 64:65], (8, HD))[None]
+                part = jnp.broadcast_to(dr[b // 2, 2][:, 64 + 32 * (b % 2):65 + 32 * (b % 2)], (8, HD))[None]
                 add = jnp.where(flag, jnp.exp2((jnp.minimum(m, top) - top) * factor), 0.0)
                 total = total + add * part
-                mixed = mixed + add * dr[b // 2, b % 2, 0][None]
+                mixed = mixed + add * dr[b // 2, b % 2][None]
             lane3 = lax.broadcasted_iota(jnp.int32, (PG, 8, HD), 2)
             cs[:, 0] = mixed
             cs[:, 1] = jnp.where(lane3 < 64, top, total)
             for g in range(PG):
                 remote(cs.at[g], dz.at[role], dout.at[3], din.at[3], line(PG + g)).start()
 
-        for j in range(HALF):
-            own(j)
-            if j < 2:
-                own_along_y(j)
+        own_wait(0)
+        own(0)
+
+        for slot in range(1, SLOTS):
+            @pl.when(chip < slot)
+            def _(slot=slot):
+                for j in range(HALF):
+                    kvbuf[j, (8 - slot) * 256:(9 - slot) * 256, :] = jnp.zeros((256, 256), jnp.bfloat16)
 
         spread_queries()
+        own_along_y(0)
 
         def start_q(h, carry):
             remote(q_columns(1 - core, h), qbuf.at[core, h], send_sem.at[11], q_sem.at[0], sibling).start()
             return carry
 
         lax.fori_loop(0, 32, start_q, 0)
+        for j in range(1, HALF):
+            own_wait(j)
         partial_terms()
+        own(1)
         inject(0)
+        own_along_y(1)
+        combine_terms()
+        forward(0)
+        own(2)
+        inject(1)
         own_along_y(2)
-        forward(0)
-        combine_terms()
-        inject(1)
-        own_along_y(3)
         rest(0)
 
         await_bytes(qbuf.at[0], q_sem.at[0])
@@ -438,9 +444,17 @@
             j = i // 2
             weave((2 * i, sbuf, peak0), (2 * i + 1, sbuf1, peak1))
 
+            @pl.when(i == 0)
+            def _():
+                own(3)
+
             @pl.when(jnp.logical_and(i % 2 == 0, j < HALF - 1))
             def _():
                 forward(j + 1)
+
+            @pl.when(i == 1)
+            def _():
+                own_along_y(3)
 
             @pl.when(jnp.logical_and(i % 2 == 1, j < HALF - 2))
             def _():
@@ -531,7 +545,8 @@
             others = [(seq + 4 * i + d) % 32 for d in range(4)]
             for other in others:
                 columns = pl.ds(pl.multiple_of(other * 256, 256), 256)
-                rs_s[other] = jnp.dot(attended, wbuf[:, columns], preferred_element_type=jnp.float32)
+                rs_s[other] = jnp.dot(
+                    attended, wbuf[:, columns], preferred_element_type=jnp.float32).astype(jnp.bfloat16)
             for other in others:
                 @pl.when(other != seq)
                 def _(other=other):
@@ -544,7 +559,7 @@
         await_bytes(rs_r.at[0:31], din.at[4])
 
         def add(i, total):
-            four = [rs_r[4 * i + d] for d in range(4)]
+            four = [rs_r[4 * i + d].astype(jnp.float32) for d in range(4)]
             return total + ((four[0] + four[1]) + (four[2] + four[3]))
 
         summed = lax.fori_loop(0, 8, add, jnp.zeros((16, 256), jnp.float32))
@@ -569,7 +584,7 @@
         fused_kernel,
         out_shape=[
             jax.ShapeDtypeStruct((BLOCK, H * HD), jnp.bfloat16),
-            jax.ShapeDtypeStruct((64, H * HD), jnp.bfloat16),
+            jax.ShapeDtypeStruct((16, 2, 64, 256), jnp.bfloat16),
         ],
         in_specs=[smem, smem, hbm, hbm, vmem, vmem, hbm],
         out_specs=[hbm, hbm],
@@ -584,13 +599,14 @@
             pltpu.VMEM((BLOCK, 1024), jnp.bfloat16),
             pltpu.VMEM((256, 8192), jnp.bfloat16),
             pltpu.VMEM((PG, 8, HD), jnp.float32),
-            pltpu.VMEM((16, PG, 8, HD), jnp.float32),
-            pltpu.VMEM((16, 2, 2, 8, HD), jnp.float32),
-            pltpu.VMEM((16, 2, 2, 8, HD), jnp.float32),
+            pltpu.VMEM((32, HD), jnp.bfloat16),
+            pltpu.VMEM((16, 32, HD), jnp.bfloat16),
+            pltpu.VMEM((16, 3, 8, HD), jnp.float32),
+            pltpu.VMEM((16, 3, 8, HD), jnp.float32),
             pltpu.VMEM((PG, 2, 8, HD), jnp.float32),
             pltpu.VMEM((PG, 2, 8, HD), jnp.float32),
-            pltpu.VMEM((32, 16, 256), jnp.float32),
-            pltpu.VMEM((32, 16, 256), jnp.float32),
+            pltpu.VMEM((32, 16, 256), jnp.bfloat16),
+            pltpu.VMEM((32, 16, 256), jnp.bfloat16),
             pltpu.VMEM((8, 16, 256), jnp.bfloat16),
             pltpu.VMEM((64, 256), jnp.bfloat16),
             pltpu.SemaphoreType.DMA((SLOTS, HALF)),
@@ -618,7 +634,8 @@
     prefill_out, decode_out = fused(
         prompt_lengths, decode_group, prefill_queries[0], prefill_kv[0], dq, fresh, out_weight
     )
-    return prefill_out[None], decode_out.reshape(4, PG, PG, -1)
+    decode_out = decode_out.reshape(32, 4, PG, PG, 256).transpose(1, 2, 3, 0, 4).reshape(4, PG, PG, -1)
+    return prefill_out[None], decode_out
 
 
 def solution(mesh):

time: 105 us -> 88.7 us (0.84)
  Pallas kernels: 97.4 us -> 80.8 us
    pallas_call x1, Pallas kernels: 97.4 us -> 80.8 us  [fused(): pl.pallas_call(fused_kernel, out_shape=[jax.ShapeDtypeStruct((BLOCK, H *...]
    reshape x1 -> x2, local copies, waits for them, and re-layouts: 2.39 us -> 2.97 us  [on_device(): decode_out.reshape(32, 4, PG, PG, 256).transpose(1, 2, 3, 0, 4)]
where the time goes in v2:
time: 88.7 us; the launch traced here: 88.4 us
  Pallas kernels  80.8 us (91%)
  local copies, waits for them, and re-layouts  6.22 us (7%)
    pallas_call x1, Pallas kernels, fused(): pl.pallas_call(fused_kernel, out_shape=[jax.ShapeDtypeStruct((BLOCK, H *...  80.8 us
    reshape x2, local copies, waits for them, and re-layouts, on_device(): decode_out.reshape(32, 4, PG, PG, 256).transpose(1, 2, 3, 0, 4)  2.97 us

profile of v2, /device:TPU:1, one launch (start us, length us, event | category | flops | bytes accessed | tf_op | source)
XLA Modules:
  0.0 88.4 jit_solution(1045629114383633745)
XLA Ops:
  0.6 0.7 bitcast_convert_fusion
  1.4 0.6 copy.16
  2.0 0.7 reshape.24
  2.7 0.6 copy.11
  3.3 80.8 %shard_map.86 = (bf16[128,8192]{1,0:T(8,128)(2,1)}, bf16[16,2,64,256]{3,2,1,0:T(8,128)(2,1)}) custom-call(s32[4,4]{1,0:T(4,128)} %lengths.1, s32[4,4]{1,0:T(4,128)} %serves.1, bf16[128,8192]{1,0:T(8,128)(2,1)} %bitcast.22, bf16[128,2048]{1,0:T(8,128)(2,1)} %bitcast.23, f32[4,8,128]{2,1,0:T(8,128)} %bitcast.21, f32[4,2,4,128]{3,2,1,0:T(4,128)} %bitcast.20, ...), custom_call_target="tpu_custom_call" | custom-call | flops 16999999488 | bytes 16000000 | tf_op jit(solution)/shard_map/pallas_call | solution.py:583
  84.1 0.0 copy-start
  84.1 1.5 %reshape.20 = bf16[32,4,4,4,256]{4,3,2,1,0:T(4,128)(2,1)S(1)} reshape(bf16[16,2,64,256]{3,2,1,0:T(8,128)(2,1)} %get-tuple-element.5) | data formatting | bytes 2097152 | tf_op jit(solution)/shard_map/reshape | solution.py:637
  85.6 1.5 %copy.14 = bf16[32,4,4,1,4,256]{5,4,0,3,2,1:T(4,128)(2,1)} copy(bf16[32,4,4,1,4,256]{5,4,3,2,1,0:T(4,128)(2,1)S(1)} %bitcast.17) | data formatting | bytes 2097152 | tf_op jit(solution)/shard_map/reshape | solution.py:637
  87.0 0.0 copy-done
  87.0 1.3 %copy.18 = bf16[1,128,8192]{2,1,0:T(8,128)(2,1)} copy(bf16[1,128,8192]{2,1,0:T(8,128)(2,1)S(1)} %bitcast.18) | data formatting | bytes 4194304
Async XLA Ops:
  84.1 3.0 %copy-start = (bf16[128,8192]{1,0:T(8,128)(2,1)S(1)}, bf16[128,8192]{1,0:T(8,128)(2,1)}, u32[]{:S(2)}) copy-start(bf16[128,8192]{1,0:T(8,128)(2,1)} %get-tuple-element.4) | copy-start | bytes 6291460

commit v3 on v2

--- a/solution.py
+++ b/solution.py
@@ -26,7 +26,7 @@
 
 def fused_kernel(
     lengths, serves, q_hbm, kv_hbm, dq, fresh, w_hbm, out_hbm, dec_hbm,
-    qbuf, kvbuf, sbuf, sbuf1, peak0, peak1, obuf, zbuf, wbuf, qz, qb, qd, ds, dr, cs, dz, rs_s, rs_r, fz, fo,
+    qbuf, kvbuf, rawbuf, stage, sbuf, sbuf1, peak0, peak1, eye, maskbuf, obuf, zbuf, wbuf, qz, qb, qd, ds, dr, cs, dz, rs_s, rs_r, fz, fo,
     slot_sem, q_sem, own_sem, out_sem, fill_sem, send_sem, din, dout, dlocal
 ):
     role = lax.axis_index("role")
@@ -55,14 +55,8 @@
     def q_columns(half, h):
         return q_hbm.at[:, pl.ds(pl.multiple_of((half * 32 + h) * HD, HD), HD)]
 
-    def kv_columns(half, j):
-        return kv_hbm.at[:, pl.ds(pl.multiple_of(half * HALF * 256 + j * 256, 256), 256)]
-
     def chunk(slot, j):
-        return kvbuf.at[j, pl.ds(pl.multiple_of((8 - slot) * 256, 256), 256), :]
-
-    def own_rows(j):
-        return kvbuf.at[j, pl.ds(pl.multiple_of(2048 + core * 128, 128), 128), :]
+        return kvbuf.at[j, pl.ds(16 - 2 * slot, 2)]
 
     barrier = pltpu.get_barrier_semaphore()
 
@@ -76,14 +70,24 @@
     def _():
         for g in range(PG):
             pl.semaphore_signal(barrier, inc=1, device_id=line(PG + g), device_id_type=MESH)
-        for j in range(HALF):
-            pltpu.make_async_copy(kv_columns(core, j), own_rows(j), own_sem.at[j]).start()
+        raw_copy = pltpu.make_async_copy(kv_hbm, rawbuf, own_sem.at[0])
+        raw_copy.start()
 
         def keep_q(h, carry):
             pltpu.make_async_copy(q_columns(core, h), qbuf.at[core, h], q_sem.at[1]).start()
             return carry
 
         lax.fori_loop(0, 32, keep_q, 0)
+        raw_copy.wait()
+
+        def halves(side, j):
+            start = pl.multiple_of(side * HALF * 256 + j * 256, 256)
+            return rawbuf[:, pl.ds(start, HD)].T, rawbuf[:, pl.ds(pl.multiple_of(start + HD, HD), HD)]
+
+        for j in range(HALF):
+            stage[j, 0], stage[j, 1] = halves(1 - core, j)
+        for j in range(HALF):
+            kvbuf[j, 16 + core, 0], kvbuf[j, 16 + core, 1] = halves(core, j)
         pl.semaphore_wait(barrier, 35)
 
     @pl.when(role >= PG)
@@ -143,7 +147,7 @@
             return plane((xx * 4 + yy) * 2 + core)
 
         for j in range(HALF):
-            remote(kv_columns(1 - core, j), own_rows(j), send_sem.at[10], slot_sem.at[0, j], sibling).start()
+            remote(stage.at[j], kvbuf.at[j, 16 + core], send_sem.at[10], slot_sem.at[0, j], sibling).start()
 
         def wait_slot(slot, j):
             @pl.when(chip >= slot)
@@ -154,8 +158,7 @@
             remote(chunk(src, j), chunk(dst, j), send_sem.at[kind], slot_sem.at[dst, j], device(xx, yy)).start()
 
         def own_wait(j):
-            pltpu.make_async_copy(kv_columns(core, j), own_rows(j), own_sem.at[j]).wait()
-            await_bytes(own_rows(j), slot_sem.at[0, j])
+            await_bytes(kvbuf.at[j, 16 + core], slot_sem.at[0, j])
 
         def own(j):
             @pl.when(x < 3)
@@ -232,7 +235,7 @@
         for e in range(2):
             block = 2 * chip + e
             first = pick(block, starts)
-            firsts.append((first - (2 * chip - 15 + e)) * 128)
+            firsts.append(first - (2 * chip - 15 + e))
             lives.append(pick(block, counts) - (block - first) * 128)
 
         at_home = home == core
@@ -280,9 +283,8 @@
                     for g in range(PG):
                         q = jnp.where(group == g, wide[:, g], q)
                     q = q.reshape(32, HD).astype(jnp.bfloat16)
-                    keys = kvbuf[j, 2048 + 128 * e:2176 + 128 * e, 0:HD]
-                    values = kvbuf[j, 2048 + 128 * e:2176 + 128 * e, HD:2 * HD]
-                    s = lax.dot_general(q, keys, (((1,), (1,)), ((), ())), preferred_element_type=jnp.float32)
+                    values = kvbuf[j, 16 + e, 1]
+                    s = jnp.dot(q, kvbuf[j, 16 + e, 0], preferred_element_type=jnp.float32)
                     s = jnp.where(lanes < live, s, NEG)
                     m = jnp.max(s, axis=1, keepdims=True)
                     w = jnp.exp2((s - m) * factor)
@@ -340,28 +342,38 @@
         own_wait(0)
         own(0)
 
+        own_along_y(0)
+
         for slot in range(1, SLOTS):
             @pl.when(chip < slot)
             def _(slot=slot):
                 for j in range(HALF):
-                    kvbuf[j, (8 - slot) * 256:(9 - slot) * 256, :] = jnp.zeros((256, 256), jnp.bfloat16)
+                    kvbuf[j, 16 - 2 * slot:18 - 2 * slot] = jnp.zeros((2, 2, 128, 128), jnp.bfloat16)
+
+        at = lax.broadcasted_iota(jnp.int32, (128, 128), 0)
+        to = lax.broadcasted_iota(jnp.int32, (128, 128), 1)
+        for i in range(ROWS // 128):
+            eye[i * 128:(i + 1) * 128, :] = (at == to).astype(jnp.bfloat16)
+        for e in range(2):
+            for w in range(15):
+                level = jnp.where(firsts[e] <= w, 0.0, NEG)
+                maskbuf[e, :, w * 128:(w + 1) * 128] = jnp.full((128, 128), level, jnp.float32).astype(jnp.bfloat16)
+            maskbuf[e, :, 1920:2048] = jnp.where(to <= at, 0.0, NEG).astype(jnp.bfloat16)
 
         spread_queries()
-        own_along_y(0)
 
         def start_q(h, carry):
             remote(q_columns(1 - core, h), qbuf.at[core, h], send_sem.at[11], q_sem.at[0], sibling).start()
             return carry
 
         lax.fori_loop(0, 32, start_q, 0)
+        inject(0)
         for j in range(1, HALF):
             own_wait(j)
+        own(1)
         partial_terms()
-        own(1)
-        inject(0)
+        forward(0)
         own_along_y(1)
-        combine_terms()
-        forward(0)
         own(2)
         inject(1)
         own_along_y(2)
@@ -370,25 +382,18 @@
         await_bytes(qbuf.at[0], q_sem.at[0])
         await_bytes(qbuf.at[0], q_sem.at[1])
 
-        lane = lax.broadcasted_iota(jnp.int32, (1, KT), 1)
-        tri = lax.broadcasted_iota(jnp.int32, (ROWS, 128), 0) % 128 >= lax.broadcasted_iota(jnp.int32, (ROWS, 128), 1)
-        row_in = lax.broadcasted_iota(jnp.int32, (ROWS, 128), 0) % 128
+        row_in = lax.broadcasted_iota(jnp.int32, (ROWS, 128), 0) & 127
         ones = jnp.ones((KT, HD), jnp.bfloat16)
-        last = WINDOW // KT - 1
 
         def place(n):
             j, u = n // 4, n % 4
             return j, u // 2, j * GROUP + (u % 2) * 4
-
-        def key_rows(j, e, kt):
-            return j, pl.ds(pl.multiple_of(128 + e * 128 + kt * KT, 128), KT)
 
         def weave(current, following):
             if following is not None:
                 n, scores, peaks = following
                 j, e, base = place(n)
-                threshold = jnp.where(e == 0, firsts[0], firsts[1])
-                q = qbuf[e, pl.ds(base, 4)].reshape(ROWS, HD)
+                q = jnp.concatenate([qbuf[e, pl.ds(base, 4)].reshape(ROWS, HD), eye[...]], axis=1)
                 peak = None
             if current is not None:
                 cn, cscores, cpeaks = current
@@ -396,25 +401,23 @@
                 total = None
             for kt in range(WINDOW // KT):
                 if following is not None:
-                    rows = key_rows(j, e, kt)
-                    s = lax.dot_general(
-                        q, kvbuf[rows[0], rows[1], 0:HD], (((1,), (1,)), ((), ())), preferred_element_type=jnp.float32)
+                    blocks_t = [kvbuf[j, 1 + e + 4 * kt + i, 0] for i in range(4)]
+                    masked_keys = jnp.concatenate(
+                        [jnp.concatenate(blocks_t, axis=1), maskbuf[e, :, kt * KT:(kt + 1) * KT]], axis=0)
+                    s = jnp.dot(q, masked_keys, preferred_element_type=jnp.float32)
                 if current is not None:
                     weights = [
                         jnp.exp2((cscores[:, kt * KT + i * 128:kt * KT + (i + 1) * 128] - cpeaks[...]) * factor)
                         for i in range(KT // 128)
                     ]
-                    rows = key_rows(cj, ce, kt)
+                    values = kvbuf[cj, pl.ds(1 + ce + 4 * kt, 4), 1].reshape(KT, HD)
                     product = jnp.dot(
                         jnp.concatenate(weights, axis=1).astype(jnp.bfloat16),
-                        jnp.concatenate([kvbuf[rows[0], rows[1], HD:2 * HD], ones], axis=1),
+                        jnp.concatenate([values, ones], axis=1),
                         preferred_element_type=jnp.float32)
                     total = product if total is None else total + product
                 if following is not None:
-                    s = s + jnp.where(lane + kt * KT >= threshold, 0.0, NEG)
                     pieces = [s[:, i * 128:(i + 1) * 128] for i in range(KT // 128)]
-                    if kt == last:
-                        pieces[-1] = jnp.where(tri, pieces[-1], NEG)
                     for i, piece in enumerate(pieces):
                         scores[:, kt * KT + i * 128:kt * KT + (i + 1) * 128] = piece
                     while len(pieces) > 1:
@@ -446,6 +449,7 @@
 
             @pl.when(i == 0)
             def _():
+                combine_terms()
                 own(3)
 
             @pl.when(jnp.logical_and(i % 2 == 0, j < HALF - 1))
@@ -476,7 +480,7 @@
         finish_pair()
         weave((jnp.int32(15), sbuf1, peak1), None)
 
-        span = kvbuf.at[:, 0:256, :]
+        span = kvbuf.at[:, 0:2]
 
         def sent(kind, condition):
             @pl.when(condition)
@@ -493,7 +497,7 @@
         sent(7, jnp.logical_and(x >= 2, y > 0))
         sent(8, chip >= right_fwd)
         sent(9, chip >= left_fwd)
-        await_bytes(kvbuf.at[:, 0:128, :], send_sem.at[10])
+        await_bytes(stage, send_sem.at[10])
         await_bytes(qbuf.at[0], send_sem.at[11])
         await_bytes(obuf.at[0], send_sem.at[12])
         await_bytes(obuf.at[0], out_sem.at[0])
@@ -590,11 +594,15 @@
         out_specs=[hbm, hbm],
         scratch_shapes=[
             pltpu.VMEM((2, 32, BLOCK, HD), jnp.bfloat16),
-            pltpu.VMEM((HALF, SLOTS * 256, 256), jnp.bfloat16),
+            pltpu.VMEM((HALF, 2 * SLOTS, 2, BLOCK, HD), jnp.bfloat16),
+            pltpu.VMEM((BLOCK, 2 * KVH * HD), jnp.bfloat16),
+            pltpu.VMEM((HALF, 2, BLOCK, HD), jnp.bfloat16),
             pltpu.VMEM((ROWS, WINDOW), jnp.float32),
             pltpu.VMEM((ROWS, WINDOW), jnp.float32),
             pltpu.VMEM((ROWS, 128), jnp.float32),
             pltpu.VMEM((ROWS, 128), jnp.float32),
+            pltpu.VMEM((ROWS, 128), jnp.bfloat16),
+            pltpu.VMEM((2, 128, WINDOW), jnp.bfloat16),
             pltpu.VMEM((2, 32, BLOCK, HD), jnp.bfloat16),
             pltpu.VMEM((BLOCK, 1024), jnp.bfloat16),
             pltpu.VMEM((256, 8192), jnp.bfloat16),

time: 88.7 us -> 86.4 us (0.974)
  Pallas kernels: 80.8 us -> 78.5 us
    pallas_call x1, Pallas kernels: 80.8 us -> 78.5 us  [fused(): pl.pallas_call(fused_kernel, out_shape=[jax.ShapeDtypeStruct((BLOCK, H *...]
where the time goes in v3:
time: 86.4 us; the launch traced here: 86.1 us
  Pallas kernels  78.5 us (91%)
  local copies, waits for them, and re-layouts  6.22 us (7%)
    pallas_call x1, Pallas kernels, fused(): pl.pallas_call(fused_kernel, out_shape=[jax.ShapeDtypeStruct((BLOCK, H *...  78.5 us
    reshape x2, local copies, waits for them, and re-layouts, on_device(): decode_out.reshape(32, 4, PG, PG, 256).transpose(1, 2, 3, 0, 4)  2.97 us

profile of v3, /device:TPU:1, one launch (start us, length us, event | category | flops | bytes accessed | tf_op | source)
XLA Modules:
  0.0 86.1 jit_solution(16242469295739351093)
XLA Ops:
  0.6 0.7 bitcast_convert_fusion
  1.4 0.6 copy.16
  2.0 0.7 reshape.24
  2.7 0.6 copy.11
  3.3 78.5 %shard_map.86 = (bf16[128,8192]{1,0:T(8,128)(2,1)}, bf16[16,2,64,256]{3,2,1,0:T(8,128)(2,1)}) custom-call(s32[4,4]{1,0:T(4,128)} %lengths.1, s32[4,4]{1,0:T(4,128)} %serves.1, bf16[128,8192]{1,0:T(8,128)(2,1)} %bitcast.22, bf16[128,2048]{1,0:T(8,128)(2,1)} %bitcast.23, f32[4,8,128]{2,1,0:T(8,128)} %bitcast.21, f32[4,2,4,128]{3,2,1,0:T(4,128)} %bitcast.20, ...), custom_call_target="tpu_custom_call" | custom-call | flops 16999999488 | bytes 16000000 | tf_op jit(solution)/shard_map/pallas_call | solution.py:587
  81.8 0.0 copy-start
  81.8 1.5 %reshape.20 = bf16[32,4,4,4,256]{4,3,2,1,0:T(4,128)(2,1)S(1)} reshape(bf16[16,2,64,256]{3,2,1,0:T(8,128)(2,1)} %get-tuple-element.5) | data formatting | bytes 2097152 | tf_op jit(solution)/shard_map/reshape | solution.py:645
  83.3 1.5 %copy.14 = bf16[32,4,4,1,4,256]{5,4,0,3,2,1:T(4,128)(2,1)} copy(bf16[32,4,4,1,4,256]{5,4,3,2,1,0:T(4,128)(2,1)S(1)} %bitcast.17) | data formatting | bytes 2097152 | tf_op jit(solution)/shard_map/reshape | solution.py:645
  84.8 0.0 copy-done
  84.8 1.3 %copy.18 = bf16[1,128,8192]{2,1,0:T(8,128)(2,1)} copy(bf16[1,128,8192]{2,1,0:T(8,128)(2,1)S(1)} %bitcast.18) | data formatting | bytes 4194304
Async XLA Ops:
  81.8 3.0 %copy-start = (bf16[128,8192]{1,0:T(8,128)(2,1)S(1)}, bf16[128,8192]{1,0:T(8,128)(2,1)}, u32[]{:S(2)}) copy-start(bf16[128,8192]{1,0:T(8,128)(2,1)} %get-tuple-element.4) | copy-start | bytes 6291460

commit v4 on v2

--- a/solution.py
+++ b/solution.py
@@ -26,7 +26,7 @@
 
 def fused_kernel(
     lengths, serves, q_hbm, kv_hbm, dq, fresh, w_hbm, out_hbm, dec_hbm,
-    qbuf, kvbuf, sbuf, sbuf1, peak0, peak1, obuf, zbuf, wbuf, qz, qb, qd, ds, dr, cs, dz, rs_s, rs_r, fz, fo,
+    qbuf, kvbuf, sbuf, sbuf1, peak0, peak1, eye, maskbuf, obuf, zbuf, wbuf, qz, qb, qd, ds, dr, cs, dz, rs_s, rs_r, fz, fo,
     slot_sem, q_sem, own_sem, out_sem, fill_sem, send_sem, din, dout, dlocal
 ):
     role = lax.axis_index("role")
@@ -232,7 +232,7 @@
         for e in range(2):
             block = 2 * chip + e
             first = pick(block, starts)
-            firsts.append((first - (2 * chip - 15 + e)) * 128)
+            firsts.append(first - (2 * chip - 15 + e))
             lives.append(pick(block, counts) - (block - first) * 128)
 
         at_home = home == core
@@ -340,41 +340,49 @@
         own_wait(0)
         own(0)
 
+        own_along_y(0)
+
         for slot in range(1, SLOTS):
             @pl.when(chip < slot)
             def _(slot=slot):
                 for j in range(HALF):
                     kvbuf[j, (8 - slot) * 256:(9 - slot) * 256, :] = jnp.zeros((256, 256), jnp.bfloat16)
 
+        at = lax.broadcasted_iota(jnp.int32, (128, 128), 0)
+        to = lax.broadcasted_iota(jnp.int32, (128, 128), 1)
+        for i in range(ROWS // 128):
+            eye[i * 128:(i + 1) * 128, :] = (at == to).astype(jnp.bfloat16)
+        for e in range(2):
+            for w in range(15):
+                level = jnp.where(firsts[e] <= w, 0.0, NEG)
+                maskbuf[e, w * 128:(w + 1) * 128, :] = jnp.full((128, 128), level, jnp.float32).astype(jnp.bfloat16)
+            maskbuf[e, 1920:2048, :] = jnp.where(at <= to, 0.0, NEG).astype(jnp.bfloat16)
+
         spread_queries()
-        own_along_y(0)
 
         def start_q(h, carry):
             remote(q_columns(1 - core, h), qbuf.at[core, h], send_sem.at[11], q_sem.at[0], sibling).start()
             return carry
 
         lax.fori_loop(0, 32, start_q, 0)
+        inject(0)
         for j in range(1, HALF):
             own_wait(j)
+        own(1)
+        own_along_y(1)
         partial_terms()
-        own(1)
-        inject(0)
-        own_along_y(1)
+        forward(0)
+        inject(1)
+        own(2)
+        own_along_y(2)
         combine_terms()
-        forward(0)
-        own(2)
-        inject(1)
-        own_along_y(2)
         rest(0)
 
         await_bytes(qbuf.at[0], q_sem.at[0])
         await_bytes(qbuf.at[0], q_sem.at[1])
 
-        lane = lax.broadcasted_iota(jnp.int32, (1, KT), 1)
-        tri = lax.broadcasted_iota(jnp.int32, (ROWS, 128), 0) % 128 >= lax.broadcasted_iota(jnp.int32, (ROWS, 128), 1)
-        row_in = lax.broadcasted_iota(jnp.int32, (ROWS, 128), 0) % 128
+        row_in = lax.broadcasted_iota(jnp.int32, (ROWS, 128), 0) & 127
         ones = jnp.ones((KT, HD), jnp.bfloat16)
-        last = WINDOW // KT - 1
 
         def place(n):
             j, u = n // 4, n % 4
@@ -387,8 +395,7 @@
             if following is not None:
                 n, scores, peaks = following
                 j, e, base = place(n)
-                threshold = jnp.where(e == 0, firsts[0], firsts[1])
-                q = qbuf[e, pl.ds(base, 4)].reshape(ROWS, HD)
+                q = jnp.concatenate([qbuf[e, pl.ds(base, 4)].reshape(ROWS, HD), eye[...]], axis=1)
                 peak = None
             if current is not None:
                 cn, cscores, cpeaks = current
@@ -397,8 +404,10 @@
             for kt in range(WINDOW // KT):
                 if following is not None:
                     rows = key_rows(j, e, kt)
+                    masked_keys = jnp.concatenate(
+                        [kvbuf[rows[0], rows[1], 0:HD], maskbuf[e, kt * KT:(kt + 1) * KT, :]], axis=1)
                     s = lax.dot_general(
-                        q, kvbuf[rows[0], rows[1], 0:HD], (((1,), (1,)), ((), ())), preferred_element_type=jnp.float32)
+                        q, masked_keys, (((1,), (1,)), ((), ())), preferred_element_type=jnp.float32)
                 if current is not None:
                     weights = [
                         jnp.exp2((cscores[:, kt * KT + i * 128:kt * KT + (i + 1) * 128] - cpeaks[...]) * factor)
@@ -411,10 +420,7 @@
                         preferred_element_type=jnp.float32)
                     total = product if total is None else total + product
                 if following is not None:
-                    s = s + jnp.where(lane + kt * KT >= threshold, 0.0, NEG)
                     pieces = [s[:, i * 128:(i + 1) * 128] for i in range(KT // 128)]
-                    if kt == last:
-                        pieces[-1] = jnp.where(tri, pieces[-1], NEG)
                     for i, piece in enumerate(pieces):
                         scores[:, kt * KT + i * 128:kt * KT + (i + 1) * 128] = piece
                     while len(pieces) > 1:
@@ -446,29 +452,33 @@
 
             @pl.when(i == 0)
             def _():
+                inject(2)
                 own(3)
-
-            @pl.when(jnp.logical_and(i % 2 == 0, j < HALF - 1))
-            def _():
-                forward(j + 1)
+                own_along_y(3)
 
             @pl.when(i == 1)
             def _():
-                own_along_y(3)
-
-            @pl.when(jnp.logical_and(i % 2 == 1, j < HALF - 2))
-            def _():
-                inject(j + 2)
-
-            @pl.when(jnp.logical_and(i % 2 == 1, j < HALF - 1))
-            def _():
-                rest(j + 1)
+                inject(3)
+                rest(1)
+
+            @pl.when(i == 3)
+            def _():
+                rest(2)
+
+            @pl.when(i == 5)
+            def _():
+                rest(3)
 
             @pl.when(i == 6)
             def _():
                 finish_own()
 
             weave((2 * i + 1, sbuf1, peak1), (2 * i + 2, sbuf, peak0))
+
+            @pl.when(i < HALF - 1)
+            def _():
+                forward(i + 1)
+
             return carry
 
         lax.fori_loop(0, 7, pair, 0)
@@ -595,6 +605,8 @@
             pltpu.VMEM((ROWS, WINDOW), jnp.float32),
             pltpu.VMEM((ROWS, 128), jnp.float32),
             pltpu.VMEM((ROWS, 128), jnp.float32),
+            pltpu.VMEM((ROWS, 128), jnp.bfloat16),
+            pltpu.VMEM((2, WINDOW, 128), jnp.bfloat16),
             pltpu.VMEM((2, 32, BLOCK, HD), jnp.bfloat16),
             pltpu.VMEM((BLOCK, 1024), jnp.bfloat16),
             pltpu.VMEM((256, 8192), jnp.bfloat16),

time: 88.7 us -> 82.5 us (0.930)
  Pallas kernels: 80.8 us -> 74.6 us
    pallas_call x1, Pallas kernels: 80.8 us -> 74.6 us  [fused(): pl.pallas_call(fused_kernel, out_shape=[jax.ShapeDtypeStruct((BLOCK, H *...]
where the time goes in v4:
time: 82.5 us; the launch traced here: 82.2 us
  Pallas kernels  74.6 us (90%)
  local copies, waits for them, and re-layouts  6.22 us (8%)
    pallas_call x1, Pallas kernels, fused(): pl.pallas_call(fused_kernel, out_shape=[jax.ShapeDtypeStruct((BLOCK, H *...  74.6 us
    reshape x2, local copies, waits for them, and re-layouts, on_device(): decode_out.reshape(32, 4, PG, PG, 256).transpose(1, 2, 3, 0, 4)  2.97 us

profile of v4, /device:TPU:1, one launch (start us, length us, event | category | flops | bytes accessed | tf_op | source)
XLA Modules:
  0.0 82.2 jit_solution(5817063702850664128)
XLA Ops:
  0.6 0.7 bitcast_convert_fusion
  1.4 0.6 copy.16
  2.0 0.7 reshape.24
  2.7 0.6 copy.11
  3.3 74.6 %shard_map.86 = (bf16[128,8192]{1,0:T(8,128)(2,1)}, bf16[16,2,64,256]{3,2,1,0:T(8,128)(2,1)}) custom-call(s32[4,4]{1,0:T(4,128)} %lengths.1, s32[4,4]{1,0:T(4,128)} %serves.1, bf16[128,8192]{1,0:T(8,128)(2,1)} %bitcast.22, bf16[128,2048]{1,0:T(8,128)(2,1)} %bitcast.23, f32[4,8,128]{2,1,0:T(8,128)} %bitcast.21, f32[4,2,4,128]{3,2,1,0:T(4,128)} %bitcast.20, ...), custom_call_target="tpu_custom_call" | custom-call | flops 16999999488 | bytes 16000000 | tf_op jit(solution)/shard_map/pallas_call | solution.py:593
  77.9 0.0 copy-start
  77.9 1.5 %reshape.20 = bf16[32,4,4,4,256]{4,3,2,1,0:T(4,128)(2,1)S(1)} reshape(bf16[16,2,64,256]{3,2,1,0:T(8,128)(2,1)} %get-tuple-element.5) | data formatting | bytes 2097152 | tf_op jit(solution)/shard_map/reshape | solution.py:649
  79.4 1.5 %copy.14 = bf16[32,4,4,1,4,256]{5,4,0,3,2,1:T(4,128)(2,1)} copy(bf16[32,4,4,1,4,256]{5,4,3,2,1,0:T(4,128)(2,1)S(1)} %bitcast.17) | data formatting | bytes 2097152 | tf_op jit(solution)/shard_map/reshape | solution.py:649
  80.9 0.0 copy-done
  80.9 1.3 %copy.18 = bf16[1,128,8192]{2,1,0:T(8,128)(2,1)} copy(bf16[1,128,8192]{2,1,0:T(8,128)(2,1)S(1)} %bitcast.18) | data formatting | bytes 4194304
Async XLA Ops:
  77.9 3.0 %copy-start = (bf16[128,8192]{1,0:T(8,128)(2,1)S(1)}, bf16[128,8192]{1,0:T(8,128)(2,1)}, u32[]{:S(2)}) copy-start(bf16[128,8192]{1,0:T(8,128)(2,1)} %get-tuple-element.4) | copy-start | bytes 6291460

commit v5 on v4

--- a/solution.py
+++ b/solution.py
@@ -20,13 +20,13 @@
 HALF = KVH // 2
 GROUP = H // KVH
 ROWS = 512
-KT = 512
+KT = 1024
 WINDOW = 2048
 
 
 def fused_kernel(
-    lengths, serves, q_hbm, kv_hbm, dq, fresh, w_hbm, out_hbm, dec_hbm,
-    qbuf, kvbuf, sbuf, sbuf1, peak0, peak1, eye, maskbuf, obuf, zbuf, wbuf, qz, qb, qd, ds, dr, cs, dz, rs_s, rs_r, fz, fo,
+    lengths, serves, q_hbm, kv_hbm, raw_q, raw_kv, w_hbm, out_hbm, dec_hbm,
+    qbuf, kvbuf, sbuf, sbuf1, peak0, peak1, eye, maskbuf, obuf, zbuf, wbuf, dq, qz, qb, qd, ds, dr, cs, dz, rs_s, rs_r, fz, fo,
     slot_sem, q_sem, own_sem, out_sem, fill_sem, send_sem, din, dout, dlocal
 ):
     role = lax.axis_index("role")
@@ -115,7 +115,8 @@
         at = lax.broadcasted_iota(jnp.int32, (64, 64), 1)
         order = (at == ((to // 4) % 4) * 16 + (to % 4) * 4 + to // 16).astype(jnp.bfloat16)
         slab = jnp.dot(order, fz[0:4].reshape(64, 256), preferred_element_type=jnp.float32)
-        fo[...] = slab.astype(jnp.bfloat16)
+        for i in range(16):
+            fo[i // 4, i % 4] = slab[4 * i:4 * i + 4].astype(jnp.bfloat16)
         pltpu.make_async_copy(fo, mine, dlocal.at[1]).start()
 
         def spread(d, carry):
@@ -516,11 +517,26 @@
     @pl.when(role >= PG)
     def _():
         group = role - PG
+        to = lax.broadcasted_iota(jnp.int32, (32, 16), 0)
+        at = lax.broadcasted_iota(jnp.int32, (32, 16), 1)
+        ordered = jnp.zeros((32, HD), jnp.float32)
+        for h in range(2):
+            chosen = jnp.logical_and((to & 7) // 4 == h, at == (to & 3) * 4 + to // 8).astype(jnp.bfloat16)
+            ordered = ordered + jnp.dot(
+                chosen, raw_q[:, h * HD:(h + 1) * HD], preferred_element_type=jnp.float32)
+        dq[...] = ordered.reshape(PG, 8, HD)
         for p in range(PG):
             remote(dq.at[p], qz.at[group], dout.at[0], din.at[0], line(p)).start()
         pltpu.make_async_copy(w_hbm, wbuf, dlocal.at[0]).wait()
         await_bytes(dz, din.at[3])
-        step = lax.broadcasted_iota(jnp.int32, (8, HD), 0) % 4
+        step = lax.broadcasted_iota(jnp.int32, (8, HD), 0) & 3
+        to = lax.broadcasted_iota(jnp.int32, (32, 16), 0)
+        at = lax.broadcasted_iota(jnp.int32, (32, 16), 1)
+        chosen = jnp.logical_and((to & 7) < 4, at == (to & 3) * 4 + to // 8).astype(jnp.bfloat16)
+        new_rows = [
+            jnp.dot(chosen, raw_kv[:, i * HD:(i + 1) * HD], preferred_element_type=jnp.float32).reshape(PG, 8, HD)
+            for i in range(2)
+        ]
         tiles = []
         for p in range(PG):
             pair = dz[p, 1]
@@ -529,7 +545,7 @@
             q = dq[p]
             scores = []
             for t in range(4):
-                s = jnp.sum(q * fresh[p, 0, t:t + 1, :], axis=1, keepdims=True)
+                s = jnp.sum(q * new_rows[0][p, t:t + 1, :], axis=1, keepdims=True)
                 scores.append(jnp.where(step >= t, jnp.broadcast_to(s, (8, HD)), NEG))
             top = m
             for s in scores:
@@ -540,7 +556,7 @@
             for t in range(4):
                 w = jnp.exp2((scores[t] - top) * factor)
                 total = total + w
-                mixed = mixed + w * fresh[p, 1, t:t + 1, :]
+                mixed = mixed + w * new_rows[1][p, t:t + 1, :]
             tiles.append(mixed / total)
         rows = jnp.concatenate(tiles, axis=0).astype(jnp.bfloat16)
         to = lax.broadcasted_iota(jnp.int32, (16, 32), 0)
@@ -594,7 +610,7 @@
         fused_kernel,
         out_shape=[
             jax.ShapeDtypeStruct((BLOCK, H * HD), jnp.bfloat16),
-            jax.ShapeDtypeStruct((16, 2, 64, 256), jnp.bfloat16),
+            jax.ShapeDtypeStruct((16, 2, 4, PG, PG, 256), jnp.bfloat16),
         ],
         in_specs=[smem, smem, hbm, hbm, vmem, vmem, hbm],
         out_specs=[hbm, hbm],
@@ -611,6 +627,7 @@
             pltpu.VMEM((BLOCK, 1024), jnp.bfloat16),
             pltpu.VMEM((256, 8192), jnp.bfloat16),
             pltpu.VMEM((PG, 8, HD), jnp.float32),
+            pltpu.VMEM((PG, 8, HD), jnp.float32),
             pltpu.VMEM((32, HD), jnp.bfloat16),
             pltpu.VMEM((16, 32, HD), jnp.bfloat16),
             pltpu.VMEM((16, 3, 8, HD), jnp.float32),
@@ -620,7 +637,7 @@
             pltpu.VMEM((32, 16, 256), jnp.bfloat16),
             pltpu.VMEM((32, 16, 256), jnp.bfloat16),
             pltpu.VMEM((8, 16, 256), jnp.bfloat16),
-            pltpu.VMEM((64, 256), jnp.bfloat16),
+            pltpu.VMEM((4, PG, PG, 256), jnp.bfloat16),
             pltpu.SemaphoreType.DMA((SLOTS, HALF)),
             pltpu.SemaphoreType.DMA((2,)),
             pltpu.SemaphoreType.DMA((HALF,)),
@@ -640,9 +657,9 @@
 
 def on_device(prefill_queries, prefill_kv, prompt_lengths, decode_group, decode_queries, decode_kv, out_weight):
     kv_head = lax.axis_index("seq") // (lax.axis_size("seq") // KVH)
-    dq = decode_queries[0].reshape(4, PG, 2, HD).transpose(1, 2, 0, 3).reshape(PG, 8, HD).astype(jnp.float32)
+    dq = decode_queries.reshape(4 * PG, 2 * HD)
     fresh = lax.dynamic_slice_in_dim(decode_kv[0], kv_head * 2 * HD, 2 * HD, 2)
-    fresh = fresh.reshape(4, PG, 2, HD).transpose(1, 2, 0, 3).astype(jnp.float32)
+    fresh = fresh.reshape(4 * PG, 2 * HD)
     prefill_out, decode_out = fused(
         prompt_lengths, decode_group, prefill_queries[0], prefill_kv[0], dq, fresh, out_weight
     )

time: 82.5 us -> 82.4 us (level)
    convert_element_type x3 -> x0, local copies, waits for them, and re-layouts: 1.93 us -> none  [the longest x2 1.32 us: on_device(): decode_queries[0].reshape(4, PG, 2, HD).transpose(1, 2, 0, 3)]
    reshape x0 -> x2, local copies, waits for them, and re-layouts: none -> 1.91 us  [the longest x1 1.3 us: on_device(): dq = decode_queries.reshape(4 * PG, 2 * HD)]
    unnamed x3 -> x5, local copies, waits for them, and re-layouts: 1.32 us -> 2.14 us
    reshape x2 -> x1, local copies, waits for them, and re-layouts: 2.97 us -> 2.83 us  [on_device(): decode_out.reshape(32, 4, PG, PG, 256).transpose(1, 2, 3, 0, 4)]
where the time goes in v5:
time: 82.4 us; the launch traced here: 82.2 us
  Pallas kernels  74.6 us (91%)
  local copies, waits for them, and re-layouts  6.89 us (8%)
    pallas_call x1, Pallas kernels, fused(): pl.pallas_call(fused_kernel, out_shape=[jax.ShapeDtypeStruct((BLOCK, H *...  74.6 us
    reshape x1, local copies, waits for them, and re-layouts, on_device(): decode_out.reshape(32, 4, PG, PG, 256).transpose(1, 2, 3, 0, 4)  2.83 us
    unnamed x5, local copies, waits for them, and re-layouts  2.14 us

profile of v5, /device:TPU:1, one launch (start us, length us, event | category | flops | bytes accessed | tf_op | source)
XLA Modules:
  0.0 82.2 jit_solution(12315626939432418549)
XLA Ops:
  0.6 0.0 copy-start
  0.7 0.8 copy-done
  1.5 0.6 reshape.19.raw_kv
  2.1 1.3 %reshape.18.raw_q = bf16[16,256]{1,0:T(8,128)(2,1)} reshape(bf16[1,4,4,256]{3,2,1,0:T(4,128)(2,1)} %param.11) | data formatting | bytes 16384 | tf_op jit(solution)/shard_map/reshape | solution.py:660
  3.4 74.6 %shard_map.86 = (bf16[128,8192]{1,0:T(8,128)(2,1)}, bf16[16,2,4,4,4,256]{5,4,3,2,1,0:T(4,128)(2,1)}) custom-call(s32[4,4]{1,0:T(4,128)} %lengths.1, s32[4,4]{1,0:T(4,128)} %serves.1, bf16[128,8192]{1,0:T(8,128)(2,1)} %bitcast.11, bf16[128,2048]{1,0:T(8,128)(2,1)} %bitcast.12, bf16[16,256]{1,0:T(8,128)(2,1)} %reshape.18.raw_q, ...), custom_call_target="tpu_custom_call" | custom-call | flops 16999999488 | bytes 16000000 | tf_op jit(solution)/shard_map/pallas_call | solution.py:609
  78.0 0.0 copy-start.1
  78.0 2.8 %copy.10 = bf16[32,4,4,1,4,256]{5,4,0,3,2,1:T(4,128)(2,1)} copy(bf16[32,4,4,1,4,256]{5,4,3,2,1,0:T(4,128)(2,1)} %bitcast.10) | data formatting | bytes 2097152 | tf_op jit(solution)/shard_map/reshape | solution.py:666
  80.8 0.0 copy-done.1
  80.8 1.3 %copy.12 = bf16[1,128,8192]{2,1,0:T(8,128)(2,1)} copy(bf16[1,128,8192]{2,1,0:T(8,128)(2,1)S(1)} %bitcast.8) | data formatting | bytes 4194304
  (1 shorter events, 0.0 us)
Async XLA Ops:
  0.6 0.8 %copy-start = (bf16[1,4,4,2048]{3,2,1,0:T(4,128)(2,1)S(1)}, bf16[1,4,4,2048]{3,2,1,0:T(4,128)(2,1)}, u32[]{:S(2)}) copy-start(bf16[1,4,4,2048]{3,2,1,0:T(4,128)(2,1)} %param.12) | copy-start | bytes 196612
  78.0 2.8 %copy-start.1 = (bf16[128,8192]{1,0:T(8,128)(2,1)S(1)}, bf16[128,8192]{1,0:T(8,128)(2,1)}, u32[]{:S(2)}) copy-start(bf16[128,8192]{1,0:T(8,128)(2,1)} %get-tuple-element.4) | copy-start | bytes 6291460

commit v6 on v5

--- a/solution.py
+++ b/solution.py
@@ -26,7 +26,7 @@
 
 def fused_kernel(
     lengths, serves, q_hbm, kv_hbm, raw_q, raw_kv, w_hbm, out_hbm, dec_hbm,
-    qbuf, kvbuf, sbuf, sbuf1, peak0, peak1, eye, maskbuf, obuf, zbuf, wbuf, dq, qz, qb, qd, ds, dr, cs, dz, rs_s, rs_r, fz, fo,
+    qbuf, kvbuf, sbuf, sbuf1, peak0, peak1, eye, maskbuf, obuf, zbuf, wbuf, vq, vkv, tall, dq, qz, qb, qd, ds, dr, cs, dz, rs_s, rs_r, fz, fo,
     slot_sem, q_sem, own_sem, out_sem, fill_sem, send_sem, din, dout, dlocal
 ):
     role = lax.axis_index("role")
@@ -90,6 +90,9 @@
     def _():
         for d in range(1, 2 * PG):
             pl.semaphore_signal(barrier, inc=1, device_id=line((role + d) % (2 * PG)), device_id_type=MESH)
+        pltpu.make_async_copy(raw_q, vq, own_sem.at[0]).start()
+        kv_part = raw_kv.at[:, :, pl.ds(pl.multiple_of(seq // 4 * 256, 256), 256)]
+        pltpu.make_async_copy(kv_part, vkv, own_sem.at[1]).start()
         pltpu.make_async_copy(w_hbm, wbuf, dlocal.at[0]).start()
         zbuf[...] = jnp.zeros_like(zbuf)
         for i in range(8):
@@ -163,10 +166,6 @@
             def _():
                 send(0, 0, 4, j, (x + 1) % 4, y)
 
-            @pl.when(x < 2)
-            def _():
-                send(1, 0, 8, j, (x + 2) % 4, y)
-
         def own_along_y(j):
             @pl.when(y < 3)
             def _():
@@ -189,6 +188,11 @@
                 send(4, 4, right_dst, j, x, right)
                 send(5, 4, left_dst, j, x, left)
 
+            @pl.when(jnp.logical_and(x >= 1, x < 3))
+            def _():
+                send(1, 4, 8, j, (x + 1) % 4, y)
+
+        def inject_far(j):
             wait_slot(8, j)
 
             @pl.when(jnp.logical_and(x >= 2, y == 3))
@@ -372,6 +376,7 @@
         own(1)
         own_along_y(1)
         partial_terms()
+        inject_far(0)
         forward(0)
         inject(1)
         own(2)
@@ -453,14 +458,20 @@
 
             @pl.when(i == 0)
             def _():
+                inject_far(1)
                 inject(2)
                 own(3)
                 own_along_y(3)
 
             @pl.when(i == 1)
             def _():
+                inject_far(2)
                 inject(3)
                 rest(1)
+
+            @pl.when(i == 2)
+            def _():
+                inject_far(3)
 
             @pl.when(i == 3)
             def _():
@@ -495,7 +506,7 @@
                 await_bytes(span, send_sem.at[kind])
 
         sent(0, x < 3)
-        sent(1, x < 2)
+        sent(1, jnp.logical_and(x >= 1, x < 3))
         sent(2, y < 3)
         sent(3, y == 0)
         sent(4, x >= 1)
@@ -517,13 +528,18 @@
     @pl.when(role >= PG)
     def _():
         group = role - PG
+        pltpu.make_async_copy(raw_q, vq, own_sem.at[0]).wait()
+        pltpu.make_async_copy(vkv, vkv, own_sem.at[1]).wait()
+        for t in range(4):
+            tall[0, 4 * t:4 * t + 4, :] = vq[t].astype(jnp.float32)
+            tall[1, 4 * t:4 * t + 4, :] = vkv[t].astype(jnp.float32)
         to = lax.broadcasted_iota(jnp.int32, (32, 16), 0)
         at = lax.broadcasted_iota(jnp.int32, (32, 16), 1)
         ordered = jnp.zeros((32, HD), jnp.float32)
         for h in range(2):
             chosen = jnp.logical_and((to & 7) // 4 == h, at == (to & 3) * 4 + to // 8).astype(jnp.bfloat16)
             ordered = ordered + jnp.dot(
-                chosen, raw_q[:, h * HD:(h + 1) * HD], preferred_element_type=jnp.float32)
+                chosen, tall[0, :, h * HD:(h + 1) * HD].astype(jnp.bfloat16), preferred_element_type=jnp.float32)
         dq[...] = ordered.reshape(PG, 8, HD)
         for p in range(PG):
             remote(dq.at[p], qz.at[group], dout.at[0], din.at[0], line(p)).start()
@@ -534,7 +550,9 @@
         at = lax.broadcasted_iota(jnp.int32, (32, 16), 1)
         chosen = jnp.logical_and((to & 7) < 4, at == (to & 3) * 4 + to // 8).astype(jnp.bfloat16)
         new_rows = [
-            jnp.dot(chosen, raw_kv[:, i * HD:(i + 1) * HD], preferred_element_type=jnp.float32).reshape(PG, 8, HD)
+            jnp.dot(
+                chosen, tall[1, :, i * HD:(i + 1) * HD].astype(jnp.bfloat16), preferred_element_type=jnp.float32
+            ).reshape(PG, 8, HD)
             for i in range(2)
         ]
         tiles = []
@@ -604,7 +622,6 @@
 
 def fused(prompt_lengths, decode_group, queries, kv, dq, fresh, out_weight):
     smem = pl.BlockSpec(memory_space=pltpu.SMEM)
-    vmem = pl.BlockSpec(memory_space=pltpu.VMEM)
     hbm = pl.BlockSpec(memory_space=pl.ANY)
     return pl.pallas_call(
         fused_kernel,
@@ -612,7 +629,7 @@
             jax.ShapeDtypeStruct((BLOCK, H * HD), jnp.bfloat16),
             jax.ShapeDtypeStruct((16, 2, 4, PG, PG, 256), jnp.bfloat16),
         ],
-        in_specs=[smem, smem, hbm, hbm, vmem, vmem, hbm],
+        in_specs=[smem, smem, hbm, hbm, hbm, hbm, hbm],
         out_specs=[hbm, hbm],
         scratch_shapes=[
             pltpu.VMEM((2, 32, BLOCK, HD), jnp.bfloat16),
@@ -626,6 +643,9 @@
             pltpu.VMEM((2, 32, BLOCK, HD), jnp.bfloat16),
             pltpu.VMEM((BLOCK, 1024), jnp.bfloat16),
             pltpu.VMEM((256, 8192), jnp.bfloat16),
+            pltpu.VMEM((4, PG, 256), jnp.bfloat16),
+            pltpu.VMEM((4, PG, 256), jnp.bfloat16),
+            pltpu.VMEM((2, 4 * PG, 256), jnp.float32),
             pltpu.VMEM((PG, 8, HD), jnp.float32),
             pltpu.VMEM((PG, 8, HD), jnp.float32),
             pltpu.VMEM((32, HD), jnp.bfloat16),
@@ -656,12 +676,8 @@
 
 
 def on_device(prefill_queries, prefill_kv, prompt_lengths, decode_group, decode_queries, decode_kv, out_weight):
-    kv_head = lax.axis_index("seq") // (lax.axis_size("seq") // KVH)
-    dq = decode_queries.reshape(4 * PG, 2 * HD)
-    fresh = lax.dynamic_slice_in_dim(decode_kv[0], kv_head * 2 * HD, 2 * HD, 2)
-    fresh = fresh.reshape(4 * PG, 2 * HD)
     prefill_out, decode_out = fused(
-        prompt_lengths, decode_group, prefill_queries[0], prefill_kv[0], dq, fresh, out_weight
+        prompt_lengths, decode_group, prefill_queries[0], prefill_kv[0], decode_queries[0], decode_kv[0], out_weight
     )
     decode_out = decode_out.reshape(32, 4, PG, PG, 256).transpose(1, 2, 3, 0, 4).reshape(4, PG, PG, -1)
     return prefill_out[None], decode_out

time: 82.4 us -> 81.9 us (level)
  local copies, waits for them, and re-layouts: 6.89 us -> 4.15 us
  Pallas kernels: 74.6 us -> 77 us
    pallas_call x1, Pallas kernels: 74.6 us -> 77 us  [fused(): pl.pallas_call(fused_kernel, out_shape=[jax.ShapeDtypeStruct((BLOCK, H *...]
    reshape x2 -> x0, local copies, waits for them, and re-layouts: 1.91 us -> none  [the longest x1 1.3 us: on_device(): dq = decode_queries.reshape(4 * PG, 2 * HD)]
    unnamed x5 -> x3, local copies, waits for them, and re-layouts: 2.14 us -> 1.32 us
where the time goes in v6:
time: 81.9 us; the launch traced here: 81.8 us
  Pallas kernels  77 us (94%)
  local copies, waits for them, and re-layouts  4.15 us (5%)
    pallas_call x1, Pallas kernels, fused(): pl.pallas_call(fused_kernel, out_shape=[jax.ShapeDtypeStruct((BLOCK, H *...  77 us
    reshape x1, local copies, waits for them, and re-layouts, on_device(): decode_out.reshape(32, 4, PG, PG, 256).transpose(1, 2, 3, 0, 4)  2.83 us

profile of v6, /device:TPU:1, one launch (start us, length us, event | category | flops | bytes accessed | tf_op | source)
XLA Modules:
  0.0 81.8 jit_solution(3227737387774808165)
XLA Ops:
  0.6 77.0 %shard_map.86 = (bf16[128,8192]{1,0:T(8,128)(2,1)}, bf16[16,2,4,4,4,256]{5,4,3,2,1,0:T(4,128)(2,1)}) custom-call(s32[4,4]{1,0:T(4,128)} %lengths.1, s32[4,4]{1,0:T(4,128)} %serves.1, bf16[128,8192]{1,0:T(8,128)(2,1)} %bitcast.13, bf16[128,2048]{1,0:T(8,128)(2,1)} %bitcast.14, bf16[4,4,256]{2,1,0:T(4,128)(2,1)} %bitcast.16, bf16[4,4,2048]{2,1,0:T(4,128)(2,1)} %bitcast.15, ...), custom_call_target="tpu_custom_call" | custom-call | flops 16999999488 | bytes 16000000 | tf_op jit(solution)/shard_map/pallas_call | solution.py:626
  77.6 0.0 copy-start
  77.6 2.8 %copy.10 = bf16[32,4,4,1,4,256]{5,4,0,3,2,1:T(4,128)(2,1)} copy(bf16[32,4,4,1,4,256]{5,4,3,2,1,0:T(4,128)(2,1)} %bitcast.12) | data formatting | bytes 2097152 | tf_op jit(solution)/shard_map/reshape | solution.py:682
  80.4 0.0 copy-done
  80.4 1.3 %copy.12 = bf16[1,128,8192]{2,1,0:T(8,128)(2,1)} copy(bf16[1,128,8192]{2,1,0:T(8,128)(2,1)S(1)} %bitcast.10) | data formatting | bytes 4194304
Async XLA Ops:
  77.6 2.8 %copy-start = (bf16[128,8192]{1,0:T(8,128)(2,1)S(1)}, bf16[128,8192]{1,0:T(8,128)(2,1)}, u32[]{:S(2)}) copy-start(bf16[128,8192]{1,0:T(8,128)(2,1)} %get-tuple-element.4) | copy-start | bytes 6291460

commit v7 on v6

--- a/solution.py
+++ b/solution.py
@@ -416,12 +416,13 @@
                         q, masked_keys, (((1,), (1,)), ((), ())), preferred_element_type=jnp.float32)
                 if current is not None:
                     weights = [
-                        jnp.exp2((cscores[:, kt * KT + i * 128:kt * KT + (i + 1) * 128] - cpeaks[...]) * factor)
+                        jnp.exp2(((cscores[:, kt * KT + i * 128:kt * KT + (i + 1) * 128] - cpeaks[...]) * factor).astype(
+                            jnp.bfloat16))
                         for i in range(KT // 128)
                     ]
                     rows = key_rows(cj, ce, kt)
                     product = jnp.dot(
-                        jnp.concatenate(weights, axis=1).astype(jnp.bfloat16),
+                        jnp.concatenate(weights, axis=1),
                         jnp.concatenate([kvbuf[rows[0], rows[1], HD:2 * HD], ones], axis=1),
                         preferred_element_type=jnp.float32)
                     total = product if total is None else total + product

time: 81.9 us -> 81.9 us (level)
  no operation moved by 1% of the time
where the time goes in v7:
time: 81.9 us; the launch traced here: 81.8 us
  Pallas kernels  77 us (94%)
  local copies, waits for them, and re-layouts  4.15 us (5%)
    pallas_call x1, Pallas kernels, fused(): pl.pallas_call(fused_kernel, out_shape=[jax.ShapeDtypeStruct((BLOCK, H *...  77 us
    reshape x1, local copies, waits for them, and re-layouts, on_device(): decode_out.reshape(32, 4, PG, PG, 256).transpose(1, 2, 3, 0, 4)  2.83 us

profile of v7, /device:TPU:1, one launch (start us, length us, event | category | flops | bytes accessed | tf_op | source)
XLA Modules:
  0.0 81.8 jit_solution(17405359263531098359)
XLA Ops:
  0.6 77.0 %shard_map.86 = (bf16[128,8192]{1,0:T(8,128)(2,1)}, bf16[16,2,4,4,4,256]{5,4,3,2,1,0:T(4,128)(2,1)}) custom-call(s32[4,4]{1,0:T(4,128)} %lengths.1, s32[4,4]{1,0:T(4,128)} %serves.1, bf16[128,8192]{1,0:T(8,128)(2,1)} %bitcast.13, bf16[128,2048]{1,0:T(8,128)(2,1)} %bitcast.14, bf16[4,4,256]{2,1,0:T(4,128)(2,1)} %bitcast.16, bf16[4,4,2048]{2,1,0:T(4,128)(2,1)} %bitcast.15, ...), custom_call_target="tpu_custom_call" | custom-call | flops 16999999488 | bytes 16000000 | tf_op jit(solution)/shard_map/pallas_call | solution.py:627
  77.6 0.0 copy-start
  77.6 2.8 %copy.10 = bf16[32,4,4,1,4,256]{5,4,0,3,2,1:T(4,128)(2,1)} copy(bf16[32,4,4,1,4,256]{5,4,3,2,1,0:T(4,128)(2,1)} %bitcast.12) | data formatting | bytes 2097152 | tf_op jit(solution)/shard_map/reshape | solution.py:683
  80.4 0.0 copy-done
  80.4 1.3 %copy.12 = bf16[1,128,8192]{2,1,0:T(8,128)(2,1)} copy(bf16[1,128,8192]{2,1,0:T(8,128)(2,1)S(1)} %bitcast.10) | data formatting | bytes 4194304
Async XLA Ops:
  77.6 2.8 %copy-start = (bf16[128,8192]{1,0:T(8,128)(2,1)S(1)}, bf16[128,8192]{1,0:T(8,128)(2,1)}, u32[]{:S(2)}) copy-start(bf16[128,8192]{1,0:T(8,128)(2,1)} %get-tuple-element.4) | copy-start | bytes 6291460

commit v8 on v6

--- a/solution.py
+++ b/solution.py
@@ -19,8 +19,8 @@
 SLOTS = 9
 HALF = KVH // 2
 GROUP = H // KVH
-ROWS = 512
-KT = 1024
+ROWS = 1024
+KT = 512
 WINDOW = 2048
 
 
@@ -391,8 +391,7 @@
         ones = jnp.ones((KT, HD), jnp.bfloat16)
 
         def place(n):
-            j, u = n // 4, n % 4
-            return j, u // 2, j * GROUP + (u % 2) * 4
+            return n // 2, n % 2, n // 2 * GROUP
 
         def key_rows(j, e, kt):
             return j, pl.ds(pl.multiple_of(128 + e * 128 + kt * KT, 128), KT)
@@ -401,7 +400,7 @@
             if following is not None:
                 n, scores, peaks = following
                 j, e, base = place(n)
-                q = jnp.concatenate([qbuf[e, pl.ds(base, 4)].reshape(ROWS, HD), eye[...]], axis=1)
+                q = jnp.concatenate([qbuf[e, pl.ds(base, GROUP)].reshape(ROWS, HD), eye[...]], axis=1)
                 peak = None
             if current is not None:
                 cn, cscores, cpeaks = current
@@ -438,8 +437,8 @@
                 live = jnp.where(ce == 0, lives[0], lives[1])
                 mixed = total[:, :HD] / total[:, HD:]
                 mixed = jnp.where(row_in < live, mixed, 0.0).astype(jnp.bfloat16)
-                obuf[ce, pl.ds(cbase, 4)] = mixed.reshape(4, BLOCK, HD)
-                for i in range(4):
+                obuf[ce, pl.ds(cbase, GROUP)] = mixed.reshape(GROUP, BLOCK, HD)
+                for i in range(GROUP):
                     columns = out_hbm.at[:, pl.ds(pl.multiple_of((core * 32 + cbase + i) * HD, HD), HD)]
 
                     @pl.when(ce == core)
@@ -451,52 +450,39 @@
                         remote(obuf.at[ce, cbase + i], columns, send_sem.at[12], out_sem.at[1], sibling).start()
 
         weave(None, (jnp.int32(0), sbuf, peak0))
+        inject_far(1)
+        inject(2)
+        own(3)
+        own_along_y(3)
+        forward(1)
 
         def pair(i, carry):
-            j = i // 2
             weave((2 * i, sbuf, peak0), (2 * i + 1, sbuf1, peak1))
 
             @pl.when(i == 0)
-            def _():
-                inject_far(1)
-                inject(2)
-                own(3)
-                own_along_y(3)
-
-            @pl.when(i == 1)
             def _():
                 inject_far(2)
                 inject(3)
-                rest(1)
-
-            @pl.when(i == 2)
-            def _():
+
+            rest(i + 1)
+            weave((2 * i + 1, sbuf1, peak1), (2 * i + 2, sbuf, peak0))
+
+            @pl.when(i == 0)
+            def _():
+                forward(2)
                 inject_far(3)
 
-            @pl.when(i == 3)
-            def _():
-                rest(2)
-
-            @pl.when(i == 5)
-            def _():
-                rest(3)
-
-            @pl.when(i == 6)
-            def _():
-                finish_own()
-
-            weave((2 * i + 1, sbuf1, peak1), (2 * i + 2, sbuf, peak0))
-
-            @pl.when(i < HALF - 1)
-            def _():
-                forward(i + 1)
+            @pl.when(i == 1)
+            def _():
+                forward(3)
 
             return carry
 
-        lax.fori_loop(0, 7, pair, 0)
-        weave((jnp.int32(14), sbuf, peak0), (jnp.int32(15), sbuf1, peak1))
+        lax.fori_loop(0, 3, pair, 0)
+        finish_own()
+        weave((jnp.int32(6), sbuf, peak0), (jnp.int32(7), sbuf1, peak1))
         finish_pair()
-        weave((jnp.int32(15), sbuf1, peak1), None)
+        weave((jnp.int32(7), sbuf1, peak1), None)
 
         span = kvbuf.at[:, 0:256, :]
 

time: 81.9 us -> 81.8 us (level)
  no operation moved by 1% of the time
where the time goes in v8:
time: 81.8 us; the launch traced here: 81.7 us
  Pallas kernels  76.9 us (94%)
  local copies, waits for them, and re-layouts  4.15 us (5%)
    pallas_call x1, Pallas kernels, fused(): pl.pallas_call(fused_kernel, out_shape=[jax.ShapeDtypeStruct((BLOCK, H *...  76.9 us
    reshape x1, local copies, waits for them, and re-layouts, on_device(): decode_out.reshape(32, 4, PG, PG, 256).transpose(1, 2, 3, 0, 4)  2.83 us

profile of v8, /device:TPU:1, one launch (start us, length us, event | category | flops | bytes accessed | tf_op | source)
XLA Modules:
  0.0 81.7 jit_solution(15058965050126333770)
XLA Ops:
  0.6 76.9 %shard_map.86 = (bf16[128,8192]{1,0:T(8,128)(2,1)}, bf16[16,2,4,4,4,256]{5,4,3,2,1,0:T(4,128)(2,1)}) custom-call(s32[4,4]{1,0:T(4,128)} %lengths.1, s32[4,4]{1,0:T(4,128)} %serves.1, bf16[128,8192]{1,0:T(8,128)(2,1)} %bitcast.13, bf16[128,2048]{1,0:T(8,128)(2,1)} %bitcast.14, bf16[4,4,256]{2,1,0:T(4,128)(2,1)} %bitcast.16, bf16[4,4,2048]{2,1,0:T(4,128)(2,1)} %bitcast.15, ...), custom_call_target="tpu_custom_call" | custom-call | flops 16999999488 | bytes 16000000 | tf_op jit(solution)/shard_map/pallas_call | solution.py:612
  77.5 0.0 copy-start
  77.5 2.8 %copy.10 = bf16[32,4,4,1,4,256]{5,4,0,3,2,1:T(4,128)(2,1)} copy(bf16[32,4,4,1,4,256]{5,4,3,2,1,0:T(4,128)(2,1)} %bitcast.12) | data formatting | bytes 2097152 | tf_op jit(solution)/shard_map/reshape | solution.py:668
  80.4 0.0 copy-done
  80.4 1.3 %copy.12 = bf16[1,128,8192]{2,1,0:T(8,128)(2,1)} copy(bf16[1,128,8192]{2,1,0:T(8,128)(2,1)S(1)} %bitcast.10) | data formatting | bytes 4194304
Async XLA Ops:
  77.5 2.8 %copy-start = (bf16[128,8192]{1,0:T(8,128)(2,1)S(1)}, bf16[128,8192]{1,0:T(8,128)(2,1)}, u32[]{:S(2)}) copy-start(bf16[128,8192]{1,0:T(8,128)(2,1)} %get-tuple-element.4) | copy-start | bytes 6291460

commit v9 on v6

--- a/solution.py
+++ b/solution.py
@@ -80,7 +80,7 @@
             pltpu.make_async_copy(kv_columns(core, j), own_rows(j), own_sem.at[j]).start()
 
         def keep_q(h, carry):
-            pltpu.make_async_copy(q_columns(core, h), qbuf.at[core, h], q_sem.at[1]).start()
+            pltpu.make_async_copy(q_columns(core, h), qbuf.at[core, h], q_sem.at[1, h // GROUP]).start()
             return carry
 
         lax.fori_loop(0, 32, keep_q, 0)
@@ -217,6 +217,8 @@
                 send(9, left_fwd, 6, j, x, left)
 
         def rest(j):
+            for side in range(2):
+                await_bytes(qbuf.at[0, 0:GROUP], q_sem.at[side, j])
             wait_slot(6 - right_fwd, j)
             wait_slot(10 - left_fwd, j)
             wait_slot(2, j)
@@ -342,10 +344,15 @@
             for g in range(PG):
                 remote(cs.at[g], dz.at[role], dout.at[3], din.at[3], line(PG + g)).start()
 
+        def start_q(h, carry):
+            remote(q_columns(1 - core, h), qbuf.at[core, h], send_sem.at[11], q_sem.at[0, h // GROUP], sibling).start()
+            return carry
+
         own_wait(0)
         own(0)
 
         own_along_y(0)
+        lax.fori_loop(0, GROUP, start_q, 0)
 
         for slot in range(1, SLOTS):
             @pl.when(chip < slot)
@@ -365,11 +372,7 @@
 
         spread_queries()
 
-        def start_q(h, carry):
-            remote(q_columns(1 - core, h), qbuf.at[core, h], send_sem.at[11], q_sem.at[0], sibling).start()
-            return carry
-
-        lax.fori_loop(0, 32, start_q, 0)
+        lax.fori_loop(GROUP, 32, start_q, 0)
         inject(0)
         for j in range(1, HALF):
             own_wait(j)
@@ -381,11 +384,7 @@
         inject(1)
         own(2)
         own_along_y(2)
-        combine_terms()
         rest(0)
-
-        await_bytes(qbuf.at[0], q_sem.at[0])
-        await_bytes(qbuf.at[0], q_sem.at[1])
 
         row_in = lax.broadcasted_iota(jnp.int32, (ROWS, 128), 0) & 127
         ones = jnp.ones((KT, HD), jnp.bfloat16)
@@ -451,6 +450,7 @@
                         remote(obuf.at[ce, cbase + i], columns, send_sem.at[12], out_sem.at[1], sibling).start()
 
         weave(None, (jnp.int32(0), sbuf, peak0))
+        combine_terms()
 
         def pair(i, carry):
             j = i // 2
@@ -659,7 +659,7 @@
             pltpu.VMEM((8, 16, 256), jnp.bfloat16),
             pltpu.VMEM((4, PG, PG, 256), jnp.bfloat16),
             pltpu.SemaphoreType.DMA((SLOTS, HALF)),
-            pltpu.SemaphoreType.DMA((2,)),
+            pltpu.SemaphoreType.DMA((2, HALF)),
             pltpu.SemaphoreType.DMA((HALF,)),
             pltpu.SemaphoreType.DMA((2,)),
             pltpu.SemaphoreType.DMA((8,)),

time: 81.9 us -> 82 us (level)
  no operation moved by 1% of the time
where the time goes in v9:
time: 82 us; the launch traced here: 81.9 us
  Pallas kernels  77.1 us (94%)
  local copies, waits for them, and re-layouts  4.15 us (5%)
    pallas_call x1, Pallas kernels, fused(): pl.pallas_call(fused_kernel, out_shape=[jax.ShapeDtypeStruct((BLOCK, H *...  77.1 us
    reshape x1, local copies, waits for them, and re-layouts, on_device(): decode_out.reshape(32, 4, PG, PG, 256).transpose(1, 2, 3, 0, 4)  2.83 us

profile of v9, /device:TPU:1, one launch (start us, length us, event | category | flops | bytes accessed | tf_op | source)
XLA Modules:
  0.0 81.9 jit_solution(8137338672177439150)
XLA Ops:
  0.6 77.1 %shard_map.86 = (bf16[128,8192]{1,0:T(8,128)(2,1)}, bf16[16,2,4,4,4,256]{5,4,3,2,1,0:T(4,128)(2,1)}) custom-call(s32[4,4]{1,0:T(4,128)} %lengths.1, s32[4,4]{1,0:T(4,128)} %serves.1, bf16[128,8192]{1,0:T(8,128)(2,1)} %bitcast.13, bf16[128,2048]{1,0:T(8,128)(2,1)} %bitcast.14, bf16[4,4,256]{2,1,0:T(4,128)(2,1)} %bitcast.16, bf16[4,4,2048]{2,1,0:T(4,128)(2,1)} %bitcast.15, ...), custom_call_target="tpu_custom_call" | custom-call | flops 16999999488 | bytes 16000000 | tf_op jit(solution)/shard_map/pallas_call | solution.py:626
  77.7 0.0 copy-start
  77.7 2.8 %copy.10 = bf16[32,4,4,1,4,256]{5,4,0,3,2,1:T(4,128)(2,1)} copy(bf16[32,4,4,1,4,256]{5,4,3,2,1,0:T(4,128)(2,1)} %bitcast.12) | data formatting | bytes 2097152 | tf_op jit(solution)/shard_map/reshape | solution.py:682
  80.5 0.0 copy-done
  80.5 1.3 %copy.12 = bf16[1,128,8192]{2,1,0:T(8,128)(2,1)} copy(bf16[1,128,8192]{2,1,0:T(8,128)(2,1)S(1)} %bitcast.10) | data formatting | bytes 4194304
Async XLA Ops:
  77.7 2.8 %copy-start = (bf16[128,8192]{1,0:T(8,128)(2,1)S(1)}, bf16[128,8192]{1,0:T(8,128)(2,1)}, u32[]{:S(2)}) copy-start(bf16[128,8192]{1,0:T(8,128)(2,1)} %get-tuple-element.4) | copy-start | bytes 6291460

commit v10 on v6

--- a/solution.py
+++ b/solution.py
@@ -481,9 +481,13 @@
             def _():
                 rest(3)
 
+            @pl.when(i == 4)
+            def _():
+                finish_own()
+
             @pl.when(i == 6)
             def _():
-                finish_own()
+                finish_pair()
 
             weave((2 * i + 1, sbuf1, peak1), (2 * i + 2, sbuf, peak0))
 
@@ -495,7 +499,6 @@
 
         lax.fori_loop(0, 7, pair, 0)
         weave((jnp.int32(14), sbuf, peak0), (jnp.int32(15), sbuf1, peak1))
-        finish_pair()
         weave((jnp.int32(15), sbuf1, peak1), None)
 
         span = kvbuf.at[:, 0:256, :]

time: 81.9 us -> 83.1 us (1.015)
  Pallas kernels: 77 us -> 78.2 us
    pallas_call x1, Pallas kernels: 77 us -> 78.2 us  [fused(): pl.pallas_call(fused_kernel, out_shape=[jax.ShapeDtypeStruct((BLOCK, H *...]
where the time goes in v10:
time: 83.1 us; the launch traced here: 83 us
  Pallas kernels  78.2 us (94%)
  local copies, waits for them, and re-layouts  4.15 us (5%)
    pallas_call x1, Pallas kernels, fused(): pl.pallas_call(fused_kernel, out_shape=[jax.ShapeDtypeStruct((BLOCK, H *...  78.2 us
    reshape x1, local copies, waits for them, and re-layouts, on_device(): decode_out.reshape(32, 4, PG, PG, 256).transpose(1, 2, 3, 0, 4)  2.83 us

profile of v10, /device:TPU:1, one launch (start us, length us, event | category | flops | bytes accessed | tf_op | source)
XLA Modules:
  0.0 83.0 jit_solution(9729229066438377924)
XLA Ops:
  0.6 78.2 %shard_map.86 = (bf16[128,8192]{1,0:T(8,128)(2,1)}, bf16[16,2,4,4,4,256]{5,4,3,2,1,0:T(4,128)(2,1)}) custom-call(s32[4,4]{1,0:T(4,128)} %lengths.1, s32[4,4]{1,0:T(4,128)} %serves.1, bf16[128,8192]{1,0:T(8,128)(2,1)} %bitcast.13, bf16[128,2048]{1,0:T(8,128)(2,1)} %bitcast.14, bf16[4,4,256]{2,1,0:T(4,128)(2,1)} %bitcast.16, bf16[4,4,2048]{2,1,0:T(4,128)(2,1)} %bitcast.15, ...), custom_call_target="tpu_custom_call" | custom-call | flops 16999999488 | bytes 16000000 | tf_op jit(solution)/shard_map/pallas_call | solution.py:629
  78.9 0.0 copy-start
  78.9 2.8 %copy.10 = bf16[32,4,4,1,4,256]{5,4,0,3,2,1:T(4,128)(2,1)} copy(bf16[32,4,4,1,4,256]{5,4,3,2,1,0:T(4,128)(2,1)} %bitcast.12) | data formatting | bytes 2097152 | tf_op jit(solution)/shard_map/reshape | solution.py:685
  81.7 0.0 copy-done
  81.7 1.3 %copy.12 = bf16[1,128,8192]{2,1,0:T(8,128)(2,1)} copy(bf16[1,128,8192]{2,1,0:T(8,128)(2,1)S(1)} %bitcast.10) | data formatting | bytes 4194304
Async XLA Ops:
  78.9 2.8 %copy-start = (bf16[128,8192]{1,0:T(8,128)(2,1)S(1)}, bf16[128,8192]{1,0:T(8,128)(2,1)}, u32[]{:S(2)}) copy-start(bf16[128,8192]{1,0:T(8,128)(2,1)} %get-tuple-element.4) | copy-start | bytes 6291460

commit v11 on v6

--- a/solution.py
+++ b/solution.py
@@ -26,7 +26,7 @@
 
 def fused_kernel(
     lengths, serves, q_hbm, kv_hbm, raw_q, raw_kv, w_hbm, out_hbm, dec_hbm,
-    qbuf, kvbuf, sbuf, sbuf1, peak0, peak1, eye, maskbuf, obuf, zbuf, wbuf, vq, vkv, tall, dq, qz, qb, qd, ds, dr, cs, dz, rs_s, rs_r, fz, fo,
+    qbuf, kvbuf, sbuf, sbuf1, peak0, peak1, obuf, zbuf, wbuf, vq, vkv, tall, dq, qz, qb, qd, ds, dr, cs, dz, rs_s, rs_r, fz, fo,
     slot_sem, q_sem, own_sem, out_sem, fill_sem, send_sem, din, dout, dlocal
 ):
     role = lax.axis_index("role")
@@ -353,16 +353,6 @@
                 for j in range(HALF):
                     kvbuf[j, (8 - slot) * 256:(9 - slot) * 256, :] = jnp.zeros((256, 256), jnp.bfloat16)
 
-        at = lax.broadcasted_iota(jnp.int32, (128, 128), 0)
-        to = lax.broadcasted_iota(jnp.int32, (128, 128), 1)
-        for i in range(ROWS // 128):
-            eye[i * 128:(i + 1) * 128, :] = (at == to).astype(jnp.bfloat16)
-        for e in range(2):
-            for w in range(15):
-                level = jnp.where(firsts[e] <= w, 0.0, NEG)
-                maskbuf[e, w * 128:(w + 1) * 128, :] = jnp.full((128, 128), level, jnp.float32).astype(jnp.bfloat16)
-            maskbuf[e, 1920:2048, :] = jnp.where(at <= to, 0.0, NEG).astype(jnp.bfloat16)
-
         spread_queries()
 
         def start_q(h, carry):
@@ -388,7 +378,8 @@
         await_bytes(qbuf.at[0], q_sem.at[1])
 
         row_in = lax.broadcasted_iota(jnp.int32, (ROWS, 128), 0) & 127
-        ones = jnp.ones((KT, HD), jnp.bfloat16)
+        lane = lax.broadcasted_iota(jnp.int32, (1, KT), 1)
+        tri = row_in >= lax.broadcasted_iota(jnp.int32, (ROWS, 128), 1)
 
         def place(n):
             j, u = n // 4, n % 4
@@ -401,19 +392,19 @@
             if following is not None:
                 n, scores, peaks = following
                 j, e, base = place(n)
-                q = jnp.concatenate([qbuf[e, pl.ds(base, 4)].reshape(ROWS, HD), eye[...]], axis=1)
+                threshold = jnp.where(e == 0, firsts[0], firsts[1]) * 128
+                q = qbuf[e, pl.ds(base, 4)].reshape(ROWS, HD)
                 peak = None
             if current is not None:
                 cn, cscores, cpeaks = current
                 cj, ce, cbase = place(cn)
                 total = None
+                parts = None
             for kt in range(WINDOW // KT):
                 if following is not None:
                     rows = key_rows(j, e, kt)
-                    masked_keys = jnp.concatenate(
-                        [kvbuf[rows[0], rows[1], 0:HD], maskbuf[e, kt * KT:(kt + 1) * KT, :]], axis=1)
                     s = lax.dot_general(
-                        q, masked_keys, (((1,), (1,)), ((), ())), preferred_element_type=jnp.float32)
+                        q, kvbuf[rows[0], rows[1], 0:HD], (((1,), (1,)), ((), ())), preferred_element_type=jnp.float32)
                 if current is not None:
                     weights = [
                         jnp.exp2((cscores[:, kt * KT + i * 128:kt * KT + (i + 1) * 128] - cpeaks[...]) * factor)
@@ -422,11 +413,16 @@
                     rows = key_rows(cj, ce, kt)
                     product = jnp.dot(
                         jnp.concatenate(weights, axis=1).astype(jnp.bfloat16),
-                        jnp.concatenate([kvbuf[rows[0], rows[1], HD:2 * HD], ones], axis=1),
-                        preferred_element_type=jnp.float32)
+                        kvbuf[rows[0], rows[1], HD:2 * HD], preferred_element_type=jnp.float32)
                     total = product if total is None else total + product
+                    while len(weights) > 1:
+                        weights = [a + b for a, b in zip(weights[::2], weights[1::2])]
+                    parts = weights[0] if parts is None else parts + weights[0]
                 if following is not None:
+                    s = s + jnp.where(lane + kt * KT >= threshold, 0.0, NEG)
                     pieces = [s[:, i * 128:(i + 1) * 128] for i in range(KT // 128)]
+                    if kt == WINDOW // KT - 1:
+                        pieces[-1] = jnp.where(tri, pieces[-1], NEG)
                     for i, piece in enumerate(pieces):
                         scores[:, kt * KT + i * 128:kt * KT + (i + 1) * 128] = piece
                     while len(pieces) > 1:
@@ -436,7 +432,7 @@
                 peaks[...] = jnp.broadcast_to(jnp.max(peak, axis=1, keepdims=True), (ROWS, 128))
             if current is not None:
                 live = jnp.where(ce == 0, lives[0], lives[1])
-                mixed = total[:, :HD] / total[:, HD:]
+                mixed = total / jnp.sum(parts, axis=1, keepdims=True)
                 mixed = jnp.where(row_in < live, mixed, 0.0).astype(jnp.bfloat16)
                 obuf[ce, pl.ds(cbase, 4)] = mixed.reshape(4, BLOCK, HD)
                 for i in range(4):
@@ -638,8 +634,6 @@
             pltpu.VMEM((ROWS, WINDOW), jnp.float32),
             pltpu.VMEM((ROWS, 128), jnp.float32),
             pltpu.VMEM((ROWS, 128), jnp.float32),
-            pltpu.VMEM((ROWS, 128), jnp.bfloat16),
-            pltpu.VMEM((2, WINDOW, 128), jnp.bfloat16),
             pltpu.VMEM((2, 32, BLOCK, HD), jnp.bfloat16),
             pltpu.VMEM((BLOCK, 1024), jnp.bfloat16),
             pltpu.VMEM((256, 8192), jnp.bfloat16),

time: 81.9 us -> 82.2 us (level)
  no operation moved by 1% of the time
where the time goes in v11:
time: 82.2 us; the launch traced here: 82.1 us
  Pallas kernels  77.3 us (94%)
  local copies, waits for them, and re-layouts  4.15 us (5%)
    pallas_call x1, Pallas kernels, fused(): pl.pallas_call(fused_kernel, out_shape=[jax.ShapeDtypeStruct((BLOCK, H *...  77.3 us
    reshape x1, local copies, waits for them, and re-layouts, on_device(): decode_out.reshape(32, 4, PG, PG, 256).transpose(1, 2, 3, 0, 4)  2.83 us

profile of v11, /device:TPU:1, one launch (start us, length us, event | category | flops | bytes accessed | tf_op | source)
XLA Modules:
  0.0 82.1 jit_solution(4370971029897856832)
XLA Ops:
  0.6 77.3 %shard_map.86 = (bf16[128,8192]{1,0:T(8,128)(2,1)}, bf16[16,2,4,4,4,256]{5,4,3,2,1,0:T(4,128)(2,1)}) custom-call(s32[4,4]{1,0:T(4,128)} %lengths.1, s32[4,4]{1,0:T(4,128)} %serves.1, bf16[128,8192]{1,0:T(8,128)(2,1)} %bitcast.13, bf16[128,2048]{1,0:T(8,128)(2,1)} %bitcast.14, bf16[4,4,256]{2,1,0:T(4,128)(2,1)} %bitcast.16, bf16[4,4,2048]{2,1,0:T(4,128)(2,1)} %bitcast.15, ...), custom_call_target="tpu_custom_call" | custom-call | flops 16999999488 | bytes 16000000 | tf_op jit(solution)/shard_map/pallas_call | solution.py:622
  78.0 0.0 copy-start
  78.0 2.8 %copy.10 = bf16[32,4,4,1,4,256]{5,4,0,3,2,1:T(4,128)(2,1)} copy(bf16[32,4,4,1,4,256]{5,4,3,2,1,0:T(4,128)(2,1)} %bitcast.12) | data formatting | bytes 2097152 | tf_op jit(solution)/shard_map/reshape | solution.py:676
  80.8 0.0 copy-done
  80.8 1.3 %copy.12 = bf16[1,128,8192]{2,1,0:T(8,128)(2,1)} copy(bf16[1,128,8192]{2,1,0:T(8,128)(2,1)S(1)} %bitcast.10) | data formatting | bytes 4194304
Async XLA Ops:
  78.0 2.8 %copy-start = (bf16[128,8192]{1,0:T(8,128)(2,1)S(1)}, bf16[128,8192]{1,0:T(8,128)(2,1)}, u32[]{:S(2)}) copy-start(bf16[128,8192]{1,0:T(8,128)(2,1)} %get-tuple-element.4) | copy-start | bytes 6291460
